TPU v7x, 256 devices: a whole 4x4x8 slice. The times are simulated.
256 devices in a mesh: frames: 64 (over x, z, core), mp: 4 (over y).
Axes of the slice: x: 4, y: 4, z: 8, core: 2. Of those that a mesh axis runs over, the one named last changes fastest.
Arguments:
- frames: bfloat16 [1024, 64, 1152], P('frames'), may hold values from -6 to 6
- keyframes: int32 [256, 16], P('frames'), may hold values from 0 to 1023, as said below
- query_states: bfloat16 [256, 32, 768], P('frames'), may hold values from -6 to 6
- w_query: bfloat16 [768, 768], P(None, 'mp'), may hold values from -1 to 1
- w_key: bfloat16 [1152, 768], P(None, 'mp'), may hold values from -1 to 1
- w_value: bfloat16 [1152, 768], P(None, 'mp'), may hold values from -0.1875 to 0.1875
- w_out: bfloat16 [768, 768], P('mp'), may hold values from -0.21875 to 0.21875
- out_grad: bfloat16 [256, 32, 768], P('frames'), may hold values from -6 to 6
Outputs:
- attended: bfloat16 [256, 32, 768], P('frames', None, 'mp')
- query_grad: bfloat16 [256, 32, 768], P('frames', None, 'mp')
- frame_grad: bfloat16 [1024, 64, 1152], P('frames', None, 'mp')
Inputs may be any that keep to these rules, and one draw needn't show every extreme that they name: `keyframes`: each entry names a frame. The 64 picks of the questions of one index of frames fall on owners (frame // 16) in groups of exactly 2: every owner gets either 0 or 2 of them.
All inputs are finite; a program needn't handle non-finite values.
Results may differ from a plain program's by a relative error of at most 0.04.
The roundings to bfloat16 on the way count: a program that leaves them out, or rounds other values in their place, can miss the bound.
Values may be sent and summed in bfloat16 or wider, within the bound.
No kernel may reach another device: no remote copies, remote signals or barrier semaphores. Data moves between devices by JAX's collectives and lax.ppermute only.
A program may use at most 128 MiB of HBM per device.

v0:
```python
import functools

import jax
import jax.numpy as jnp
from jax import lax
from jax.experimental import pallas as pl
from jax.experimental.pallas import tpu as pltpu
from jax.sharding import PartitionSpec as P

HEAD_DIM = 64
NT = (((1,), (1,)), ((), ()))
TN = (((0,), (0,)), ((), ()))
NN = (((1,), (0,)), ((), ()))
F32 = jnp.float32
BF16 = jnp.bfloat16


def dot(a, b, dims):
    return lax.dot_general(a, b, dims, preferred_element_type=F32)


def head_masks(heads, wide):
    lane = lax.broadcasted_iota(jnp.int32, (1, wide), 1) // HEAD_DIM
    low = [(lane == h).astype(BF16) for h in range(heads)]
    high = [(lane == h + 1).astype(BF16) for h in range(heads)]
    return low, high


def spread(block, masks):
    return jnp.concatenate([block * m for m in masks], axis=0)


def gathered(block, masks, nq):
    total = block[:nq] * masks[0].astype(F32)
    for h in range(1, len(masks)):
        total = total + block[h * nq:(h + 1) * nq] * masks[h].astype(F32)
    return total


AXES = (4, 8, 2)
FIRST = 3


def frames_perm(dx=0, dz=0, dc=0):
    nx, nz, nc = AXES
    pairs = []
    for x in range(nx):
        for z in range(nz):
            for c in range(nc):
                to = (((x + dx) % nx) * nz + (z + dz) % nz) * nc + (c + dc) % nc
                pairs.append(((x * nz + z) * nc + c, to))
    return pairs


def planes():
    nx, nz, nc = AXES
    number = lambda x, z, c: (x * nz + z) * nc + c
    flat = [[number(x, z, c) for x in range(nx) for c in range(nc)] for z in range(nz)]
    line = [[number(x, z, c) for z in range(nz)] for x in range(nx) for c in range(nc)]
    return flat, line


def hop(value, **shift):
    return lax.ppermute(value, "frames", frames_perm(**shift))


def plan_kernel(codes_ref, me_ref, order_ref, size_ref, at_ref, *, cap, quests, nq, tok, frames_here):
    nx, nz, nc = AXES
    owners = nx * nz * nc
    bits = frames_here.bit_length() - 1
    me = me_ref[0]
    x, z, c = lax.div(me, nz * nc), lax.rem(lax.div(me, nc), nz), lax.rem(me, nc)

    def step(block, found):
        at, core, across = lax.div(block, nc * nx), lax.rem(lax.div(block, nx), nc), lax.rem(block, nx)
        away = jnp.where(lax.rem(at, 2) == 1, lax.div(at + 1, 2), nz - lax.div(at, 2))
        there = lax.rem(x - across + nx, nx) * nz + lax.rem(z - away + nz, nz)
        src = there * nc + lax.rem(c + core, nc)
        asks = (lax.rem(there, nz) * nx + lax.div(there, nz)) * nc + lax.rem(c + core, nc)
        valid = codes_ref[asks * cap] > 0
        order_ref[jnp.where(valid, found, owners - 1 - (block - found))] = src
        for r in range(cap):
            code = jnp.maximum(codes_ref[asks * cap + r] - 1, 0)
            row = (block * quests + (code >> bits)) * nq
            at_ref[src * cap + r] = jnp.where(valid, row, 0)
            at_ref[(owners + src) * cap + r] = (code & (frames_here - 1)) * tok
        return found + jnp.where(valid, 1, 0)

    near = lax.fori_loop(0, FIRST * nx * nc, step, 0)
    size_ref[1] = near
    size_ref[0] = lax.fori_loop(FIRST * nx * nc, owners, step, near)


def load_rows(pieces, x_ref, sems):
    copies, row = [], 0
    full = pieces[0].shape[0]
    for i, piece in enumerate(pieces):
        size = piece.shape[0]
        if size == full:
            row = i * full
        else:
            half, core = divmod(i - (len(pieces) - 4), 2)
            row = (len(pieces) - 4 + core) * full + half * size
        copies.append(pltpu.make_async_copy(piece, x_ref.at[pl.ds(row, size)], sems.at[i]))
        copies[-1].start()
    return copies


def in_groups(order_ref, size_ref, copies, group, step):
    early = size_ref[1] // group
    for c in copies[:2 * FIRST]:
        c.wait()
    lax.fori_loop(0, early, step, 0)
    for c in copies[2 * FIRST:]:
        c.wait()
    last = (size_ref[0] + group - 1) // group
    lax.fori_loop(early, last, step, 0)
    return last


def group_of(i, group, cap, order_ref):
    srcs = [order_ref[i * group + g] for g in range(group)]
    return srcs, [src * cap + r for src in srcs for r in range(cap)]


def rows_of(at_ref, slots, x_ref, kv_ref, nq, tok, low, high):
    at = [pl.multiple_of(at_ref[slot], nq) for slot in slots]
    keys = [pl.multiple_of(at_ref[at_ref.shape[0] // 2 + slot], tok) for slot in slots]
    qm = [spread(x_ref[pl.ds(a, nq), 0:256], low) for a in at]
    dm = [spread(x_ref[pl.ds(a, nq), 128:384], high) for a in at]
    k = [kv_ref[pl.ds(a, tok), 0:256] for a in keys]
    v = [kv_ref[pl.ds(a, tok), 128:384] for a in keys]
    s = [dot(a, b, NT) for a, b in zip(k, qm)]
    dp = [dot(a, b, NT) for a, b in zip(v, dm)]
    return s, dp, qm, dm, k, v, keys


def stats_kernel(order_ref, size_ref, at_ref, kv_ref, *refs, cap, nq, tok, heads, group):
    *pieces, out_ref, x_ref, sems = refs
    low, high = head_masks(heads, 256)
    copies = load_rows(pieces, x_ref, sems)
    wide = heads * nq

    def step(i, carry):
        srcs, slots = group_of(i, group, cap, order_ref)
        s, dp, *_ = rows_of(at_ref, slots, x_ref, kv_ref, nq, tok, low, high)
        m = [jnp.max(a, axis=0, keepdims=True) for a in s]
        e = [jnp.exp(a - b) for a, b in zip(s, m)]
        for n, (a, b, c) in enumerate(zip(m, e, dp)):
            src, r = srcs[n // cap], 3 * (n % cap)
            out_ref[src, r:r + 1, 0:wide] = a
            out_ref[src, r + 1:r + 2, 0:wide] = jnp.sum(b, axis=0, keepdims=True)
            out_ref[src, r + 2:r + 3, 0:wide] = jnp.sum(b * c, axis=0, keepdims=True)
        return carry

    in_groups(order_ref, size_ref, copies, group, step)


def combine_kernel(quest_ref, st_ref, out_ref, *, cap, quests):
    ids = [quest_ref[r] for r in range(cap)]
    top = [st_ref[:, 3 * r, :] for r in range(cap)]
    size = [st_ref[:, 3 * r + 1, :] for r in range(cap)]
    mean = [st_ref[:, 3 * r + 2, :] for r in range(cap)]
    none = jnp.zeros_like(top[0])
    outs = [[none + 3e38, none, none] for _ in range(cap)]
    for j in range(quests):
        on = [ids[r] == j for r in range(cap)]
        big = functools.reduce(
            jnp.maximum,
            [jnp.max(jnp.where(on[r], top[r], -jnp.inf), axis=0, keepdims=True) for r in range(cap)],
        )
        norm, delta = 0.0, 0.0
        for r in range(cap):
            e = jnp.exp(top[r] - big)
            norm = norm + jnp.sum(jnp.where(on[r], e * size[r], 0.0), axis=0, keepdims=True)
            delta = delta + jnp.sum(jnp.where(on[r], e * mean[r], 0.0), axis=0, keepdims=True)
        inv = 1.0 / norm
        for r in range(cap):
            for i, val in enumerate((big, inv, delta * inv)):
                outs[r][i] = jnp.where(on[r], val, outs[r][i])
    for r in range(cap):
        for i in range(3):
            out_ref[:, 3 * r + i, :] = outs[r][i]


def main_kernel(
    order_ref, size_ref, at_ref, kv_ref, st_ref, x_ref, ret_ref, sum_ref, acc_ref,
    *, cap, nq, tok, heads, group, scale
):
    low, high = head_masks(heads, 256)
    acc_ref[...] = jnp.zeros_like(acc_ref)
    wide = heads * nq
    size = cap * nq

    nx, nz, nc = AXES

    def place(src):
        column = lax.div(src, nz * nc) * nc + lax.rem(src, nc)
        return pl.multiple_of((column * nz + lax.rem(lax.div(src, nc), nz)) * size, size)

    def step(i, carry):
        srcs, slots = group_of(i, group, cap, order_ref)
        s, dp, qm, dm, k, v, keys = rows_of(at_ref, slots, x_ref, kv_ref, nq, tok, low, high)
        st = [
            [st_ref[src, 3 * r + n:3 * r + n + 1, 0:wide] for n in range(3)] for src in srcs for r in range(cap)
        ]
        p = [jnp.exp(a - b[0]) * b[1] for a, b in zip(s, st)]
        w = [a.astype(BF16) for a in p]
        ds = [(a * (b - c[2])).astype(BF16) for a, b, c in zip(p, dp, st)]
        o = [gathered(dot(a, b, TN), high, nq) for a, b in zip(w, v)]
        dq = [gathered(dot(a, b, TN), low, nq) * scale for a, b in zip(ds, k)]
        dk = [dot(a, b, NN) for a, b in zip(ds, qm)]
        dv = [dot(a, b, NN) for a, b in zip(w, dm)]
        for n in range(len(slots)):
            row = pl.ds(pl.multiple_of(place(srcs[n // cap]) + n % cap * nq, nq), nq)
            ret_ref[row, 0:128] = dq[n][:, 0:128].astype(BF16)
            ret_ref[row, 128:256] = (dq[n][:, 128:256] + o[n][:, 0:128]).astype(BF16)
            ret_ref[row, 256:384] = o[n][:, 128:256].astype(BF16)
            at = pl.ds(keys[n], tok)
            acc_ref[at, 0:128] += dk[n][:, 0:128]
            acc_ref[at, 128:256] += dk[n][:, 128:256] + dv[n][:, 0:128]
            acc_ref[at, 256:384] += dv[n][:, 128:256]
        return carry

    last = (size_ref[0] + group - 1) // group
    lax.fori_loop(0, last, step, 0)

    def rest(i, carry):
        src = order_ref[i]
        ret_ref[pl.ds(place(src), size), :] = jnp.zeros((size, ret_ref.shape[1]), BF16)
        return carry

    lax.fori_loop(last * group, order_ref.shape[0], rest, 0)
    sum_ref[...] = acc_ref[...].astype(BF16)


def merge_kernel(me_ref, pick_ref, ret_ref, *out_refs):
    nz = len(out_refs)
    for s, out_ref in enumerate(out_refs):
        to = lax.rem(me_ref[0] + s, nz)
        rows = jnp.concatenate([ret_ref[u, to] for u in range(ret_ref.shape[0])], axis=0)
        out_ref[...] = dot(pick_ref[to], rows, NN).astype(BF16)


def project_kernel(x_ref, w_ref, out_ref, *, cols):
    lane = lax.broadcasted_iota(jnp.int32, (1, 256), 1)
    grad = x_ref[:, 0:256] * (lane < cols).astype(BF16)
    mixed = x_ref[:, 128:384] * (lane >= cols - 128).astype(BF16)
    rows = x_ref.shape[0]
    many = out_ref.shape[0]
    part = w_ref.shape[0] // many
    for to in range(many):
        at = pl.ds(to * part, part)
        out_ref[to, 0:rows, :] = dot(mixed, w_ref[at, 128:384], NT).astype(out_ref.dtype)
        out_ref[to, rows:2 * rows, :] = dot(grad, w_ref[at, 0:256], NT).astype(out_ref.dtype)


def call(kernel, out_shape, ins, outs, scratch=(), mib=1):
    spaces = {"s": pltpu.SMEM, "v": pltpu.VMEM, "a": pltpu.HBM}
    out_specs = [pl.BlockSpec(memory_space=spaces[i]) for i in outs]
    return pl.pallas_call(
        kernel,
        out_shape=out_shape,
        in_specs=[pl.BlockSpec(memory_space=spaces[i]) for i in ins],
        out_specs=out_specs if len(outs) > 1 else out_specs[0],
        scratch_shapes=list(scratch),
        compiler_params=pltpu.CompilerParams(vmem_limit_bytes=mib * 1024 * 1024),
    )


def mp_hop(value, s):
    many = lax.axis_size("mp")
    return lax.ppermute(value, "mp", [(i, (i + s) % many) for i in range(many)])


def body(frames, keyframes, query_states, w_query, w_key, w_value, w_out, out_grad):
    owners = lax.axis_size("frames")
    shards = lax.axis_size("mp")
    me, shard = lax.axis_index("frames"), lax.axis_index("mp")
    fr_count, tok, width = frames.shape
    quests, keys = keyframes.shape
    nq = query_states.shape[1]
    hid = query_states.shape[2]
    cols = w_key.shape[1]
    heads = cols // HEAD_DIM
    scale = HEAD_DIM ** (-0.5)
    count = quests * keys
    cap = max(2, count // owners)
    group = 4

    queries = jnp.dot(query_states.reshape(quests * nq, hid), w_query, preferred_element_type=F32)
    d_mixed = lax.dot_general(out_grad.reshape(quests * nq, hid), w_out, NT, preferred_element_type=F32)
    local = jnp.concatenate([queries.astype(BF16) * scale, d_mixed.astype(BF16)], axis=1)
    picks = keyframes.reshape(-1)
    owner = picks >> (fr_count.bit_length() - 1)
    position = jnp.arange(count)
    same = owner[:, None] == owner[None, :]
    rank = jnp.sum(jnp.logical_and(same, position[None, :] < position[:, None]), axis=1)
    code = (picks & (fr_count - 1)) + fr_count * (position // keys) + 1
    slot = owner * cap + rank
    requests = jnp.sum(
        jnp.where(slot[None, :] == jnp.arange(owners * cap)[:, None], code[None, :], 0), axis=1
    ).astype(jnp.int32)
    asked = jnp.where(requests > 0, (requests - 1) >> (fr_count.bit_length() - 1), -1)
    quest_of = jnp.broadcast_to(asked.reshape(owners, cap).T[:, :, None], (cap, owners, 128))

    nx, nz, nc = AXES
    owners = nx * nz * nc
    bits = frames_here.bit_length() - 1
    me = me_ref[0]
    x, z, c = lax.div(me, nz * nc), lax.rem(lax.div(me, nc), nz), lax.rem(me, nc)

    def step(block, found):
        at, core, across = lax.div(block, nc * nx), lax.rem(lax.div(block, nx), nc), lax.rem(block, nx)
        away = jnp.where(lax.rem(at, 2) == 1, lax.div(at + 1, 2), nz - lax.div(at, 2))
        there = lax.rem(x - across + nx, nx) * nz + lax.rem(z - away + nz, nz)
        src = there * nc + lax.rem(c + core, nc)
        asks = (lax.rem(there, nz) * nx + lax.div(there, nz)) * nc + lax.rem(c + core, nc)
        valid = codes_ref[asks * cap] > 0
        order_ref[jnp.where(valid, found, owners - 1 - (block - found))] = src
        for r in range(cap):
            code = jnp.maximum(codes_ref[asks * cap + r] - 1, 0)
            row = (block * quests + (code >> bits)) * nq
            at_ref[src * cap + r] = jnp.where(valid, row, 0)
            at_ref[(owners + src) * cap + r] = (code & (frames_here - 1)) * tok
        return found + jnp.where(valid, 1, 0)

    near = lax.fori_loop(0, FIRST * nx * nc, step, 0)
    size_ref[1] = near
    size_ref[0] = lax.fori_loop(FIRST * nx * nc, owners, step, near)


def load_rows(pieces, x_ref, sems):
    copies, row = [], 0
    full = pieces[0].shape[0]
    for i, piece in enumerate(pieces):
        size = piece.shape[0]
        if size == full:
            row = i * full
        else:
            half, core = divmod(i - (len(pieces) - 4), 2)
            row = (len(pieces) - 4 + core) * full + half * size
        copies.append(pltpu.make_async_copy(piece, x_ref.at[pl.ds(row, size)], sems.at[i]))
        copies[-1].start()
    return copies


def in_groups(order_ref, size_ref, copies, group, step):
    early = size_ref[1] // group
    for c in copies[:2 * FIRST]:
        c.wait()
    lax.fori_loop(0, early, step, 0)
    for c in copies[2 * FIRST:]:
        c.wait()
    last = (size_ref[0] + group - 1) // group
    lax.fori_loop(early, last, step, 0)
    return last


def group_of(i, group, cap, order_ref):
    srcs = [order_ref[i * group + g] for g in range(group)]
    return srcs, [src * cap + r for src in srcs for r in range(cap)]


def rows_of(at_ref, slots, x_ref, kv_ref, nq, tok, low, high):
    at = [pl.multiple_of(at_ref[slot], nq) for slot in slots]
    keys = [pl.multiple_of(at_ref[at_ref.shape[0] // 2 + slot], tok) for slot in slots]
    qm = [spread(x_ref[pl.ds(a, nq), 0:256], low) for a in at]
    dm = [spread(x_ref[pl.ds(a, nq), 128:384], high) for a in at]
    k = [kv_ref[pl.ds(a, tok), 0:256] for a in keys]
    v = [kv_ref[pl.ds(a, tok), 128:384] for a in keys]
    s = [dot(a, b, NT) for a, b in zip(k, qm)]
    dp = [dot(a, b, NT) for a, b in zip(v, dm)]
    return s, dp, qm, dm, k, v, keys


def stats_kernel(order_ref, size_ref, at_ref, kv_ref, *refs, cap, nq, tok, heads, group):
    *pieces, out_ref, x_ref, sems = refs
    low, high = head_masks(heads, 256)
    copies = load_rows(pieces, x_ref, sems)
    wide = heads * nq

    def step(i, carry):
        srcs, slots = group_of(i, group, cap, order_ref)
        s, dp, *_ = rows_of(at_ref, slots, x_ref, kv_ref, nq, tok, low, high)
        m = [jnp.max(a, axis=0, keepdims=True) for a in s]
        e = [jnp.exp(a - b) for a, b in zip(s, m)]
        for n, (a, b, c) in enumerate(zip(m, e, dp)):
            src, r = srcs[n // cap], 3 * (n % cap)
            out_ref[src, r:r + 1, 0:wide] = a
            out_ref[src, r + 1:r + 2, 0:wide] = jnp.sum(b, axis=0, keepdims=True)
            out_ref[src, r + 2:r + 3, 0:wide] = jnp.sum(b * c, axis=0, keepdims=True)
        return carry

    in_groups(order_ref, size_ref, copies, group, step)


def combine_kernel(quest_ref, st_ref, out_ref, *, cap, quests):
    ids = [quest_ref[r] for r in range(cap)]
    top = [st_ref[:, 3 * r, :] for r in range(cap)]
    size = [st_ref[:, 3 * r + 1, :] for r in range(cap)]
    mean = [st_ref[:, 3 * r + 2, :] for r in range(cap)]
    none = jnp.zeros_like(top[0])
    outs = [[none + 3e38, none, none] for _ in range(cap)]
    for j in range(quests):
        on = [ids[r] == j for r in range(cap)]
        big = functools.reduce(
            jnp.maximum,
            [jnp.max(jnp.where(on[r], top[r], -jnp.inf), axis=0, keepdims=True) for r in range(cap)],
        )
        norm, delta = 0.0, 0.0
        for r in range(cap):
            e = jnp.exp(top[r] - big)
            norm = norm + jnp.sum(jnp.where(on[r], e * size[r], 0.0), axis=0, keepdims=True)
            delta = delta + jnp.sum(jnp.where(on[r], e * mean[r], 0.0), axis=0, keepdims=True)
        inv = 1.0 / norm
        for r in range(cap):
            for i, val in enumerate((big, inv, delta * inv)):
                outs[r][i] = jnp.where(on[r], val, outs[r][i])
    for r in range(cap):
        for i in range(3):
            out_ref[:, 3 * r + i, :] = outs[r][i]


def main_kernel(
    order_ref, size_ref, at_ref, kv_ref, st_ref, x_ref, ret_ref, sum_ref, acc_ref,
    *, cap, nq, tok, heads, group, scale
):
    low, high = head_masks(heads, 256)
    acc_ref[...] = jnp.zeros_like(acc_ref)
    wide = heads * nq
    size = cap * nq

    nx, nz, nc = AXES

    def place(src):
        column = lax.div(src, nz * nc) * nc + lax.rem(src, nc)
        return pl.multiple_of((column * nz + lax.rem(lax.div(src, nc), nz)) * size, size)

    def step(i, carry):
        srcs, slots = group_of(i, group, cap, order_ref)
        s, dp, qm, dm, k, v, keys = rows_of(at_ref, slots, x_ref, kv_ref, nq, tok, low, high)
        st = [
            [st_ref[src, 3 * r + n:3 * r + n + 1, 0:wide] for n in range(3)] for src in srcs for r in range(cap)
        ]
        p = [jnp.exp(a - b[0]) * b[1] for a, b in zip(s, st)]
        w = [a.astype(BF16) for a in p]
        ds = [(a * (b - c[2])).astype(BF16) for a, b, c in zip(p, dp, st)]
        o = [gathered(dot(a, b, TN), high, nq) for a, b in zip(w, v)]
        dq = [gathered(dot(a, b, TN), low, nq) * scale for a, b in zip(ds, k)]
        dk = [dot(a, b, NN) for a, b in zip(ds, qm)]
        dv = [dot(a, b, NN) for a, b in zip(w, dm)]
        for n in range(len(slots)):
            row = pl.ds(pl.multiple_of(place(srcs[n // cap]) + n % cap * nq, nq), nq)
            ret_ref[row, 0:128] = dq[n][:, 0:128].astype(BF16)
            ret_ref[row, 128:256] = (dq[n][:, 128:256] + o[n][:, 0:128]).astype(BF16)
            ret_ref[row, 256:384] = o[n][:, 128:256].astype(BF16)
            at = pl.ds(keys[n], tok)
            acc_ref[at, 0:128] += dk[n][:, 0:128]
            acc_ref[at, 128:256] += dk[n][:, 128:256] + dv[n][:, 0:128]
            acc_ref[at, 256:384] += dv[n][:, 128:256]
        return carry

    last = (size_ref[0] + group - 1) // group
    lax.fori_loop(0, last, step, 0)

    def rest(i, carry):
        src = order_ref[i]
        ret_ref[pl.ds(place(src), size), :] = jnp.zeros((size, ret_ref.shape[1]), BF16)
        return carry

    lax.fori_loop(last * group, order_ref.shape[0], rest, 0)
    sum_ref[...] = acc_ref[...].astype(BF16)


def merge_kernel(me_ref, pick_ref, ret_ref, *out_refs):
    nz = len(out_refs)
    for s, out_ref in enumerate(out_refs):
        to = lax.rem(me_ref[0] + s, nz)
        rows = jnp.concatenate([ret_ref[u, to] for u in range(ret_ref.shape[0])], axis=0)
        out_ref[...] = dot(pick_ref[to], rows, NN).astype(BF16)


def finish_kernel(*refs, cols):
    *ins, att_ref, grad_ref = refs
    many = len(ins) // 2
    lane = lax.broadcasted_iota(jnp.int32, (1, 256), 1)
    low = (lane < cols).astype(BF16)
    high = (lane >= cols - 128).astype(BF16)
    att, grad = 0.0, 0.0
    for x_ref, w_ref in zip(ins[:many], ins[many:]):
        grad = grad + dot(x_ref[:, 0:256] * low, w_ref[:, 0:256], NT)
        att = att + dot(x_ref[:, 128:384] * high, w_ref[:, 128:384], NT)
    att_ref[...] = att.astype(BF16)
    grad_ref[...] = grad.astype(BF16)


def call(kernel, out_shape, ins, outs, scratch=(), mib=1):
    spaces = {"s": pltpu.SMEM, "v": pltpu.VMEM, "a": pltpu.HBM}
    out_specs = [pl.BlockSpec(memory_space=spaces[i]) for i in outs]
    return pl.pallas_call(
        kernel,
        out_shape=out_shape,
        in_specs=[pl.BlockSpec(memory_space=spaces[i]) for i in ins],
        out_specs=out_specs if len(outs) > 1 else out_specs[0],
        scratch_shapes=list(scratch),
        compiler_params=pltpu.CompilerParams(vmem_limit_bytes=mib * 1024 * 1024),
    )


def mp_hop(value, s):
    many = lax.axis_size("mp")
    return lax.ppermute(value, "mp", [(i, (i + s) % many) for i in range(many)])


def body(frames, keyframes, query_states, w_query, w_key, w_value, w_out, out_grad):
    owners = lax.axis_size("frames")
    shards = lax.axis_size("mp")
    me, shard = lax.axis_index("frames"), lax.axis_index("mp")
    fr_count, tok, width = frames.shape
    quests, keys = keyframes.shape
    nq = query_states.shape[1]
    hid = query_states.shape[2]
    cols = w_key.shape[1]
    heads = cols // HEAD_DIM
    scale = HEAD_DIM ** (-0.5)
    count = quests * keys
    cap = max(2, count // owners)
    group = 4

    queries = jnp.dot(query_states.reshape(quests * nq, hid), w_query, preferred_element_type=F32)
    d_mixed = lax.dot_general(out_grad.reshape(quests * nq, hid), w_out, NT, preferred_element_type=F32)
    local = jnp.concatenate([queries.astype(BF16) * scale, d_mixed.astype(BF16)], axis=1)
    picks = keyframes.reshape(-1)
    owner = picks >> (fr_count.bit_length() - 1)
    position = jnp.arange(count)
    same = owner[:, None] == owner[None, :]
    rank = jnp.sum(jnp.logical_and(same, position[None, :] < position[:, None]), axis=1)
    code = (picks & (fr_count - 1)) + fr_count * (position // keys) + 1
    slot = owner * cap + rank
    requests = jnp.sum(
        jnp.where(slot[None, :] == jnp.arange(owners * cap)[:, None], code[None, :], 0), axis=1
    ).astype(jnp.int32)
    asked = jnp.where(requests > 0, (requests - 1) >> (fr_count.bit_length() - 1), -1)
    quest_of = jnp.broadcast_to(asked.reshape(owners, cap).T[:, :, None], (cap, owners, 128))
    put = jnp.arange(quests * nq)[:, None]
    take = jnp.arange(owners * cap * nq)[None, :]
    pick_sum = jnp.logical_and(put // nq == jnp.repeat(asked, nq)[None, :], put % nq == take % nq).astype(BF16)

    w_both = jnp.concatenate([w_key, w_value], axis=1)
    bank = jnp.dot(frames.reshape(fr_count * tok, width), w_both, preferred_element_type=F32).astype(BF16)
    flat, line = planes()
    nx, nz, nc = AXES
    mine = jnp.concatenate([local] + [hop(local, dx=s) for s in range(1, nx)], axis=0)
    passed = requests.reshape(nx, nz, nc, cap).swapaxes(0, 1).reshape(nz, nx * nc * cap)
    passed = lax.all_to_all(passed, "frames", 0, 0, axis_index_groups=line, tiled=True)
    mine, passed, bank = lax.optimization_barrier((mine, passed, bank))
    incoming = passed.reshape(nz, nx * nc, cap).swapaxes(0, 1).reshape(nx * nc, nz * cap)
    incoming = lax.all_to_all(incoming, "frames", 0, 0, axis_index_groups=flat, tiled=True)
    incoming = incoming.reshape(nx * nc, nz, cap).swapaxes(0, 1).reshape(-1)
    ways = [(mine, mine)]
    ways.append((hop(ways[-1][0], dz=1), hop(ways[-1][1], dz=-1)))
    ways[-1], incoming = lax.optimization_barrier((ways[-1], incoming))
    ints = lambda *shape: jax.ShapeDtypeStruct(shape, jnp.int32)
    order, sizes, at = call(
        functools.partial(plan_kernel, cap=cap, quests=quests, nq=nq, tok=tok, frames_here=fr_count),
        (ints(owners), ints(2), ints(2 * owners * cap)),
        "ss",
        "sss",
    )(incoming, me.astype(jnp.int32).reshape(1))
    ways.append((hop(ways[-1][0], dz=1), hop(ways[-1][1], dz=-1)))
    ways[-1], order, sizes, at, quest_of = lax.optimization_barrier((ways[-1], order, sizes, at, quest_of))
    ways.append((hop(ways[-1][0], dz=1), hop(ways[-1][1], dz=-1)))
    half = mine.shape[0] // 2
    pieces = [mine] + [way for pair in ways[1:] for way in pair]
    pieces += [hop(ways[-1][0][:half], dz=1), hop(ways[-1][1][half:], dz=-1)]
    pieces = [p for piece in pieces for p in (piece, hop(piece, dc=1))]

    dims = dict(cap=cap, nq=nq, tok=tok, heads=heads, group=group)
    held = (owners * cap * nq, 2 * cols)
    stat_shape = jax.ShapeDtypeStruct((owners, 8, 128), F32)
    rows = jax.ShapeDtypeStruct((owners * quests * nq, 2 * cols), BF16)
    stats, rows = call(
        functools.partial(stats_kernel, **dims),
        (stat_shape, rows),
        "sssv" + "a" * len(pieces),
        "vv",
        [pltpu.SemaphoreType.DMA((len(pieces),))],
        4,
    )(order, sizes, at, bank, *pieces)
    stats = lax.all_to_all(stats, "frames", split_axis=0, concat_axis=0, tiled=True)
    stats = call(functools.partial(combine_kernel, cap=cap, quests=quests), stat_shape, "vv", "v")(quest_of, stats)
    stats = lax.all_to_all(stats, "frames", split_axis=0, concat_axis=0, tiled=True)
    partial, sums = call(
        functools.partial(main_kernel, scale=scale, **dims),
        (jax.ShapeDtypeStruct(held, BF16), jax.ShapeDtypeStruct((fr_count * tok, 2 * cols), BF16)),
        "sssvvv",
        "vv",
        [pltpu.VMEM((fr_count * tok, 2 * cols), F32)],
        8,
    )(order, sizes, at, bank, stats, rows)
    partial = lax.all_to_all(
        partial.reshape(nx * nc, nz * cap * nq, 2 * cols), "frames", 0, 0, axis_index_groups=flat, tiled=True
    ).reshape(nx * nc, nz, cap * nq, 2 * cols)
    asked = jnp.where(passed > 0, (passed - 1) >> (fr_count.bit_length() - 1), -1)
    put = jnp.arange(quests * nq)[None, :, None]
    take = jnp.arange(nx * nc * cap * nq)[None, None, :]
    asked = jnp.repeat(asked.reshape(nz, 1, nx * nc * cap), nq, axis=2)
    pick_sum = jnp.logical_and(put // nq == asked, put % nq == take % nq).astype(BF16)

    w_q_out = jnp.concatenate([w_query, w_out.T], axis=1)
    own = [(shard + s) % shards for s in range(shards)]
    part = hid // shards
    slab = width // shards
    terms = [
        lax.dot_general(
            sums, lax.dynamic_slice_in_dim(w_both, own[s] * slab, slab, 0), NT, preferred_element_type=F32
        )
        for s in range(shards)
    ]
    frame_grad = terms[0]
    for s in range(1, shards):
        frame_grad = frame_grad + mp_hop(terms[s].astype(BF16), s).astype(F32)

    frame_grad = frame_grad.astype(BF16).reshape(fr_count, tok, slab)
    partial, w_q_out, pick_sum = lax.optimization_barrier((partial, w_q_out, pick_sum))
    mine_shape = jax.ShapeDtypeStruct((quests * nq, 2 * cols), BF16)
    merged = call(merge_kernel, (mine_shape,) * nz, "svv", "v" * nz, mib=4)(
        lax.rem(lax.div(me, nc), nz).astype(jnp.int32).reshape(1), pick_sum, partial
    )
    mine = merged[0].astype(F32)
    for s in range(1, nz):
        mine = mine + hop(merged[s], dz=s).astype(F32)
    mine, frame_grad = lax.optimization_barrier((mine.astype(BF16), frame_grad))
    blocks = call(
        functools.partial(project_kernel, cols=cols),
        jax.ShapeDtypeStruct((shards, 2 * quests * nq, part), BF16),
        "vv",
        "v",
        mib=2,
    )(mine, w_q_out)
    blocks = lax.all_to_all(blocks, "mp", 0, 0, tiled=True)
    both = jnp.sum(blocks.astype(F32), axis=0).astype(BF16).reshape(2, quests, nq, part)
    return both[0], both[1], frame_grad


def solution(mesh):
    placed = (
        P("frames", None, None),
        P("frames", None),
        P("frames", None, None),
        P(None, "mp"),
        P(None, "mp"),
        P(None, "mp"),
        P("mp", None),
        P("frames", None, None),
    )
    return jax.shard_map(
        body,
        mesh=mesh,
        in_specs=placed,
        out_specs=(P("frames", None, "mp"), P("frames", None, "mp"), P("frames", None, "mp")),
        check_vma=False,
    )
```

profile of v0, /device:TPU:1, one launch (start us, length us, event | category | flops | bytes accessed | tf_op | source)
XLA Modules:
  0.0 221.9 jit_solution(10420458547942937568)
XLA Ops:
  0.7 1.4 convolution_convert_fusion.4
  2.3 1.3 convolution_convert_fusion.5
  4.4 3.4 %collective-permute-start.2 = (bf16[128,384]{1,0:T(8,128)(2,1)S(1)}, bf16[128,384]{1,0:T(8,128)(2,1)S(1)}, u32[]{:S(2)}, u32[]{:S(2)}) collective-permute-start(bf16[128,384]{1,0:T(8,128)(2,1)S(1)} %pad_maximum_fusion.2), channel_id=1, source_target_pairs={{0,192},{4,196},{8,200},{12,204},{16,208},{20,212},{24,216},{28,22... | collective-permute-start | bytes 294920 | tf_op jit(solution)/shard_map/ppermute | solution.py:64
  10.1 0.7 copy.104
  10.8 8.2 %all-to-all-start = ((s32[8,1,16]{2,1,0:T(1,128)}), s32[8,1,16]{2,1,0:T(1,128)S(1)}, u32[]{:S(2)}, u32[]{:S(2)}) async-start(s32[8,1,16]{2,1,0:T(1,128)} %copy.104), calls=%async_computation | async-start | bytes 8192 | tf_op jit(solution)/shard_map/all_to_all | solution.py:556
  19.2 1.5 fusion.3.kv_ref
  20.7 0.7 copy-done.16
  21.4 1.1 pad_maximum_fusion.1.refs_0_
  22.5 3.1 %all-to-all-done = s32[8,1,16]{2,1,0:T(1,128)S(1)} async-done(((s32[8,1,16]{2,1,0:T(1,128)}), s32[8,1,16]{2,1,0:T(1,128)S(1)}, u32[]{:S(2)}, u32[]{:S(2)}) %all-to-all-start) | async-done | bytes 544 | tf_op jit(solution)/shard_map/all_to_all | solution.py:556
  25.8 2.4 %collective-permute-start.4 = (bf16[512,384]{1,0:T(8,128)(2,1)S(1)}, bf16[512,384]{1,0:T(8,128)(2,1)}, u32[]{:S(2)}, u32[]{:S(2)}) collective-permute-start(bf16[512,384]{1,0:T(8,128)(2,1)S(1)} %pad_maximum_fusion.1.refs_0_), channel_id=1, source_target_pairs={{0,56},{4,60},{8,0},{12,4},{16,8},{20,12},{24,16},{28,20},{32,24},... | collective-permute-start | bytes 1179656 | tf_op jit(solution)/shard_map/ppermute | solution.py:64
  28.2 0.7 copy.106
  28.9 0.8 copy.107
  29.7 11.4 %all_to_all.41 = s32[8,1,16]{2,1,0:T(1,128)} all-to-all(s32[8,1,16]{2,1,0:T(1,128)S(1)} %copy.108), channel_id=1, replica_groups={{0,4,64,68,128,132,192,196},{8,12,72,76,136,140,200,204},{16,20,80,84,1..., dimensions={0} | all-to-all | bytes 1024 | tf_op jit(solution)/shard_map/all_to_all | solution.py:559
  41.2 0.7 copy.109
  41.9 0.7 copy.110
  42.6 0.9 reshape.221.codes_ref
  43.7 2.7 %collective-permute-start.6 = (bf16[512,384]{1,0:T(8,128)(2,1)}, bf16[512,384]{1,0:T(8,128)(2,1)}, u32[]{:S(2)}, u32[]{:S(2)}) collective-permute-start(bf16[512,384]{1,0:T(8,128)(2,1)} %collective-permute-done.4.refs_4_), channel_id=1, source_target_pairs={{0,56},{4,60},{8,0},{12,4},{16,8},{20,12},{24,16},{28,20},{32,24},... | collective-permute-start | bytes 1179656 | tf_op jit(solution)/shard_map/ppermute | solution.py:64
  46.3 0.7 and_select_fusion
  47.0 0.8 select_n.91
  47.7 0.8 copy.111
  48.6 3.6 %shard_map.103 = (s32[64]{0:T(128)S(1)}, s32[2]{0:T(128)S(1)}, s32[256]{0:T(256)S(1)}) custom-call(s32[128]{0:T(128)S(1)} %reshape.221.codes_ref, s32[1]{0:T(128)} %bitcast.13.me_ref), custom_call_target="tpu_custom_call" | custom-call | tf_op jit(solution)/shard_map/pallas_call | solution.py:565
  52.2 3.1 %collective-permute-done.5.refs_6_ = bf16[512,384]{1,0:T(8,128)(2,1)} collective-permute-done((bf16[512,384]{1,0:T(8,128)(2,1)}, bf16[512,384]{1,0:T(8,128)(2,1)}, u32[]{:S(2)}, u32[]{:S(2)}) %collective-permute-start.5) | collective-permute-done | bytes 393248 | tf_op jit(solution)/shard_map/ppermute | solution.py:64
  55.4 2.7 %collective-permute-start.14 = (bf16[512,384]{1,0:T(8,128)(2,1)}, bf16[512,384]{1,0:T(8,128)(2,1)S(1)}, u32[]{:S(2)}, u32[]{:S(2)}) collective-permute-start(bf16[512,384]{1,0:T(8,128)(2,1)} %collective-permute-done.6.refs_8_), channel_id=1, source_target_pairs={{0,56},{4,60},{8,0},{12,4},{16,8},{20,12},{24,16},{28,20},{32,24},... | collective-permute-start | bytes 1179656 | tf_op jit(solution)/shard_map/ppermute | solution.py:64
  58.1 2.0 collective-permute-start.7
  60.6 5.5 %collective-permute-done.12.refs_10_ = bf16[512,384]{1,0:T(8,128)(2,1)S(1)} collective-permute-done((bf16[512,384]{1,0:T(8,128)(2,1)}, bf16[512,384]{1,0:T(8,128)(2,1)S(1)}, u32[]{:S(2)}, u32[]{:S(2)}) %collective-permute-start.12) | collective-permute-done | bytes 393248 | tf_op jit(solution)/shard_map/ppermute | solution.py:64
  66.1 2.3 %collective-permute-start.10 = (bf16[512,384]{1,0:T(8,128)(2,1)}, bf16[512,384]{1,0:T(8,128)(2,1)S(1)}, u32[]{:S(2)}, u32[]{:S(2)}) collective-permute-start(bf16[512,384]{1,0:T(8,128)(2,1)} %collective-permute-done.5.refs_6_), channel_id=1, source_target_pairs={{0,4},{4,0},{8,12},{12,8},{16,20},{20,16},{24,28},{28,24},{32,36},... | collective-permute-start | bytes 1179656 | tf_op jit(solution)/shard_map/ppermute | solution.py:64
  69.9 2.4 %collective-permute-start.18 = (bf16[256,384]{1,0:T(8,128)(2,1)S(1)}, bf16[256,384]{1,0:T(8,128)(2,1)S(1)}, u32[]{:S(2)}, u32[]{:S(2)}) collective-permute-start(bf16[256,384]{1,0:T(8,128)(2,1)S(1)} %slice.19), channel_id=1, source_target_pairs={{0,56},{4,60},{8,0},{12,4},{16,8},{20,12},{24,16},{28,20},{32,24},... | collective-permute-start | bytes 589832 | tf_op jit(solution)/shard_map/ppermute | solution.py:64
  72.4 3.6 %collective-permute-done.16.refs_14_ = bf16[256,384]{1,0:T(8,128)(2,1)S(1)} collective-permute-done((bf16[256,384]{1,0:T(8,128)(2,1)S(1)}, bf16[256,384]{1,0:T(8,128)(2,1)S(1)}, u32[]{:S(2)}, u32[]{:S(2)}) %collective-permute-start.16) | collective-permute-done | bytes 196640 | tf_op jit(solution)/shard_map/ppermute | solution.py:64
  76.0 1.3 collective-permute-start.17
  77.5 0.9 collective-permute-done.17.refs_15_
  78.8 6.8 %shard_map.104 = (f32[64,8,128]{2,1,0:T(8,128)S(1)}, bf16[8192,384]{1,0:T(8,128)(2,1)S(1)}) custom-call(s32[64]{0:T(128)S(1)} %get-tuple-element.43.order_ref, s32[2]{0:T(128)S(1)} %get-tuple-element.44.size_ref, s32[256]{0:T(256)S(1)} %get-tuple-element.45.at_ref, bf16[1024,384]{1,0:T(8,128)(2,1)S(1)} %fusion.3.kv_ref, ...), custom_call_target="tpu_custom_call" | custom-call | tf_op jit(solution)/shard_map/pallas_call | solution.py:583
  85.6 19.0 %all_to_all.42.st_ref = f32[64,8,128]{2,1,0:T(8,128)S(1)} all-to-all(f32[64,8,128]{2,1,0:T(8,128)S(1)} %get-tuple-element.50), channel_id=1, replica_groups=mesh['frames'=64,'mp'=4] {'frames'}, dimensions={0} | all-to-all | bytes 524288 | tf_op jit(solution)/shard_map/all_to_all | solution.py:591
  105.0 17.8 %all_to_all.43.st_ref = f32[64,8,128]{2,1,0:T(8,128)S(1)} all-to-all(f32[64,8,128]{2,1,0:T(8,128)S(1)} %shard_map.105), channel_id=1, replica_groups=mesh['frames'=64,'mp'=4] {'frames'}, dimensions={0} | all-to-all | bytes 524288 | tf_op jit(solution)/shard_map/all_to_all | solution.py:593
  122.9 6.9 %shard_map.106 = (bf16[4096,384]{1,0:T(8,128)(2,1)S(1)}, bf16[1024,384]{1,0:T(8,128)(2,1)S(1)}) custom-call(s32[64]{0:T(128)S(1)} %get-tuple-element.43.order_ref, s32[2]{0:T(128)S(1)} %get-tuple-element.44.size_ref, s32[256]{0:T(256)S(1)} %get-tuple-element.45.at_ref, bf16[1024,384]{1,0:T(8,128)(2,1)S(1)} %copy-done.4, ...), custom_call_target="tpu_custom_call" | custom-call | tf_op jit(solution)/shard_map/pallas_call | solution.py:594
  129.8 1.7 copy-done.2
  131.4 5.9 %all-to-all-start.4 = ((bf16[8,512,384]{2,1,0:T(8,128)(2,1)}), bf16[8,512,384]{2,1,0:T(8,128)(2,1)}, u32[]{:S(2)}, u32[]{:S(2)}) async-start(bf16[8,512,384]{2,1,0:T(8,128)(2,1)} %bitcast.35), calls=%async_computation.4 | async-start | bytes 6291456 | tf_op jit(solution)/shard_map/all_to_all | solution.py:602
  137.3 1.1 copy.112
  138.5 1.9 copy.113
  140.4 2.2 pad_maximum_fusion.w_ref
  142.6 1.4 convolution_convert_fusion.1
  144.1 2.7 %collective-permute-start.29 = (bf16[1024,288]{0,1:T(8,128)(2,1)}, bf16[1024,288]{0,1:T(8,128)(2,1)}, u32[]{:S(2)}, u32[]{:S(2)}) collective-permute-start(bf16[1024,288]{0,1:T(8,128)(2,1)} %convolution_convert_fusion.1), channel_id=1, source_target_pairs={{0,3},{1,0},{2,1},{3,2},{4,7},{5,4},{6,5},{7,6},{8,11},{9,8},{10,9... | collective-permute-start | bytes 1769480 | tf_op jit(solution)/shard_map/ppermute | solution.py:513
  146.8 1.4 convolution_convert_fusion.2
  148.5 1.4 convolution_convert_fusion.3
  150.0 0.7 collective-permute-start.27
  150.9 1.4 and_convert_fusion.pick_ref
  152.3 22.8 %all-to-all-done.4 = bf16[8,512,384]{2,1,0:T(8,128)(2,1)} async-done(((bf16[8,512,384]{2,1,0:T(8,128)(2,1)}), bf16[8,512,384]{2,1,0:T(8,128)(2,1)}, u32[]{:S(2)}, u32[]{:S(2)}) %all-to-all-start.4) | async-done | bytes 3145760 | tf_op jit(solution)/shard_map/all_to_all | solution.py:602
  175.0 1.2 copy-done.1
  176.2 3.2 %shard_map.107 = (bf16[128,384]{1,0:T(8,128)(2,1)S(1)}, bf16[128,384]{1,0:T(8,128)(2,1)S(1)}, bf16[128,384]{1,0:T(8,128)(2,1)S(1)}, bf16[128,384]{1,0:T(8,128)(2...) custom-call(s32[1]{0:T(128)} %bitcast.me_ref, ...), custom_call_target="tpu_custom_call" | custom-call | tf_op jit(solution)/shard_map/pallas_call | solution.py:628
  179.5 0.6 copy-done.6
  180.7 1.2 collective-permute-start.26
  181.9 1.6 collective-permute-start.25
  183.5 3.0 %collective-permute-start.24 = (bf16[128,384]{1,0:T(8,128)(2,1)}, bf16[128,384]{1,0:T(8,128)(2,1)}, u32[]{:S(2)}, u32[]{:S(2)}) collective-permute-start(bf16[128,384]{1,0:T(8,128)(2,1)} %copy-done.7), channel_id=1, source_target_pairs={{0,40},{4,44},{8,48},{12,52},{16,56},{20,60},{24,0},{28,4},{32,8},... | collective-permute-start | bytes 294920 | tf_op jit(solution)/shard_map/ppermute | solution.py:64
  186.5 2.6 %collective-permute-start.23 = (bf16[128,384]{1,0:T(8,128)(2,1)}, bf16[128,384]{1,0:T(8,128)(2,1)}, u32[]{:S(2)}, u32[]{:S(2)}) collective-permute-start(bf16[128,384]{1,0:T(8,128)(2,1)} %copy-done.6), channel_id=1, source_target_pairs={{0,32},{4,36},{8,40},{12,44},{16,48},{20,52},{24,56},{28,60},{32,0... | collective-permute-start | bytes 294920 | tf_op jit(solution)/shard_map/ppermute | solution.py:64
  189.2 0.8 collective-permute-start.22
  190.0 1.9 collective-permute-start.21
  192.3 3.0 %fusion.2 = bf16[1024,288]{0,1:T(8,128)(2,1)} fusion(bf16[1024,384]{1,0:T(8,128)(2,1)S(1)} %get-tuple-element.63, bf16[1024,288]{0,1:T(8,128)(2,1)} %collective-permute-done.29, bf16[1024,288]{0,1:T(8,128)(2,1)} %collective-permute-done.28, bf16[1024,288]{0,1:T(8,128)(2,1)} %collective-permute-done.27, bf16[1152,384]{0,1:T(8,128)(2,1)} %copy-done.8, ...), kind=kOutput, calls=%fused_computation.5 | convolution fusion | flops 228556800 | bytes 3440644 | tf_op jit(solution)/shard_map/dot_general | solution.py:616
  195.3 2.3 %copy.114 = bf16[1024,288]{1,0:T(8,128)(2,1)} copy(bf16[1024,288]{0,1:T(8,128)(2,1)} %fusion.2) | data formatting | bytes 1179648 | tf_op jit(solution)/shard_map/convert_element_type | solution.py:625
  198.0 5.5 %collective-permute-done.22 = bf16[128,384]{1,0:T(8,128)(2,1)} collective-permute-done((bf16[128,384]{1,0:T(8,128)(2,1)S(1)}, bf16[128,384]{1,0:T(8,128)(2,1)}, u32[]{:S(2)}, u32[]{:S(2)}) %collective-permute-start.22) | collective-permute-done | bytes 98336 | tf_op jit(solution)/shard_map/ppermute | solution.py:64
  203.5 3.7 %collective-permute-done.20 = bf16[128,384]{1,0:T(8,128)(2,1)} collective-permute-done((bf16[128,384]{1,0:T(8,128)(2,1)S(1)}, bf16[128,384]{1,0:T(8,128)(2,1)}, u32[]{:S(2)}, u32[]{:S(2)}) %collective-permute-start.20) | collective-permute-done | bytes 98336 | tf_op jit(solution)/shard_map/ppermute | solution.py:64
  207.2 1.3 add_convert_fusion.x_ref
  208.9 0.9 copy.115
  209.8 10.5 %all_to_all.44 = bf16[4,256,192]{1,2,0:T(8,128)(2,1)S(1)} all-to-all(bf16[4,256,192]{1,2,0:T(8,128)(2,1)} %copy.115), channel_id=1, replica_groups=mesh['frames'=64,'mp'=4] {'mp'}, dimensions={0} | all-to-all | bytes 786432 | tf_op jit(solution)/shard_map/all_to_all | solution.py:642
  220.4 0.7 copy.116
  221.1 0.7 copy.117
  (101 shorter events, 9.4 us)
Async XLA Ops:
  0.6 18.5 %copy-start = (bf16[16,64,1152]{2,1,0:T(8,128)(2,1)S(1)}, bf16[16,64,1152]{2,1,0:T(8,128)(2,1)}, u32[]{:S(2)}) copy-start(bf16[16,64,1152]{2,1,0:T(8,128)(2,1)} %param.8) | copy-start | bytes 7077892
  0.6 8.3 %copy-start.17 = (s32[4,16]{1,0:T(4,128)S(1)}, s32[4,16]{1,0:T(4,128)}, u32[]{:S(2)}) copy-start(s32[4,16]{1,0:T(4,128)} %param.9) | copy-start | bytes 772
  0.7 18.3 %copy-start.14 = (bf16[1152,192]{0,1:T(8,128)(2,1)S(1)}, bf16[1152,192]{0,1:T(8,128)(2,1)}, u32[]{:S(2)}) copy-start(bf16[1152,192]{0,1:T(8,128)(2,1)} %param.12) | copy-start | bytes 1327108
  2.1 16.9 %copy-start.15 = (bf16[1152,192]{0,1:T(8,128)(2,1)S(1)}, bf16[1152,192]{0,1:T(8,128)(2,1)}, u32[]{:S(2)}) copy-start(bf16[1152,192]{0,1:T(8,128)(2,1)} %param.13) | copy-start | bytes 1327108
  2.2 16.9 %copy-start.10 = (bf16[128,192]{1,0:T(8,128)(2,1)}, bf16[128,192]{1,0:T(8,128)(2,1)S(1)}, u32[]{:S(2)}) copy-start(bf16[128,192]{1,0:T(8,128)(2,1)S(1)} %copy.102) | copy-start | bytes 147460
  3.7 0.6 copy-start.12
  4.4 16.2 %collective-permute-start.2 = (bf16[128,384]{1,0:T(8,128)(2,1)S(1)}, bf16[128,384]{1,0:T(8,128)(2,1)S(1)}, u32[]{:S(2)}, u32[]{:S(2)}) collective-permute-start(bf16[128,384]{1,0:T(8,128)(2,1)S(1)} %pad_maximum_fusion.2), channel_id=1, source_target_pairs={{0,192},{4,196},{8,200},{12,204},{16,208},{20,212},{24,216},{28,22... | collective-permute-start | bytes 294920 | tf_op jit(solution)/shard_map/ppermute | solution.py:64
  7.8 12.8 %collective-permute-start.1 = (bf16[128,384]{1,0:T(8,128)(2,1)S(1)}, bf16[128,384]{1,0:T(8,128)(2,1)}, u32[]{:S(2)}, u32[]{:S(2)}) collective-permute-start(bf16[128,384]{1,0:T(8,128)(2,1)S(1)} %pad_maximum_fusion.2), channel_id=1, source_target_pairs={{0,128},{4,132},{8,136},{12,140},{16,144},{20,148},{24,152},{28,15... | collective-permute-start | bytes 294920 | tf_op jit(solution)/shard_map/ppermute | solution.py:64
  8.3 13.0 %collective-permute-start = (bf16[128,384]{1,0:T(8,128)(2,1)S(1)}, bf16[128,384]{1,0:T(8,128)(2,1)}, u32[]{:S(2)}, u32[]{:S(2)}) collective-permute-start(bf16[128,384]{1,0:T(8,128)(2,1)S(1)} %pad_maximum_fusion.2), channel_id=1, source_target_pairs={{0,64},{4,68},{8,72},{12,76},{16,80},{20,84},{24,88},{28,92},{32,9... | collective-permute-start | bytes 294920 | tf_op jit(solution)/shard_map/ppermute | solution.py:64
  9.4 0.6 copy-start.18
  10.8 14.7 %all-to-all-start = ((s32[8,1,16]{2,1,0:T(1,128)}), s32[8,1,16]{2,1,0:T(1,128)S(1)}, u32[]{:S(2)}, u32[]{:S(2)}) async-start(s32[8,1,16]{2,1,0:T(1,128)} %copy.104), calls=%async_computation | async-start | bytes 8192 | tf_op jit(solution)/shard_map/all_to_all | solution.py:556
  19.1 1.5 copy-start.8
  19.1 2.2 %copy-start.11 = (bf16[128,192]{1,0:T(8,128)(2,1)S(1)}, bf16[128,192]{1,0:T(8,128)(2,1)}, u32[]{:S(2)}) copy-start(bf16[128,192]{1,0:T(8,128)(2,1)} %copy-done.10) | copy-start | bytes 147460
  19.1 2.2 %copy-start.13 = (bf16[128,192]{1,0:T(8,128)(2,1)S(1)}, bf16[128,192]{1,0:T(8,128)(2,1)}, u32[]{:S(2)}) copy-start(bf16[128,192]{1,0:T(8,128)(2,1)} %copy-done.12) | copy-start | bytes 147460
  20.6 65.0 %copy-start.3 = (bf16[1024,384]{1,0:T(8,128)(2,1)}, bf16[1024,384]{1,0:T(8,128)(2,1)S(1)}, u32[]{:S(2)}) copy-start(bf16[1024,384]{1,0:T(8,128)(2,1)S(1)} %fusion.3.kv_ref) | copy-start | bytes 2359300
  20.6 0.7 copy-start.16
  25.5 18.0 %collective-permute-start.3 = (bf16[512,384]{1,0:T(8,128)(2,1)S(1)}, bf16[512,384]{1,0:T(8,128)(2,1)}, u32[]{:S(2)}, u32[]{:S(2)}) collective-permute-start(bf16[512,384]{1,0:T(8,128)(2,1)S(1)} %pad_maximum_fusion.1.refs_0_), channel_id=1, source_target_pairs={{0,8},{4,12},{8,16},{12,20},{16,24},{20,28},{24,32},{28,36},{32,40... | collective-permute-start | bytes 1179656 | tf_op jit(solution)/shard_map/ppermute | solution.py:64
  25.8 17.7 %collective-permute-start.4 = (bf16[512,384]{1,0:T(8,128)(2,1)S(1)}, bf16[512,384]{1,0:T(8,128)(2,1)}, u32[]{:S(2)}, u32[]{:S(2)}) collective-permute-start(bf16[512,384]{1,0:T(8,128)(2,1)S(1)} %pad_maximum_fusion.1.refs_0_), channel_id=1, source_target_pairs={{0,56},{4,60},{8,0},{12,4},{16,8},{20,12},{24,16},{28,20},{32,24},... | collective-permute-start | bytes 1179656 | tf_op jit(solution)/shard_map/ppermute | solution.py:64
  43.6 11.7 %collective-permute-start.5 = (bf16[512,384]{1,0:T(8,128)(2,1)}, bf16[512,384]{1,0:T(8,128)(2,1)}, u32[]{:S(2)}, u32[]{:S(2)}) collective-permute-start(bf16[512,384]{1,0:T(8,128)(2,1)} %collective-permute-done.3.refs_2_), channel_id=1, source_target_pairs={{0,8},{4,12},{8,16},{12,20},{16,24},{20,28},{24,32},{28,36},{32,40... | collective-permute-start | bytes 1179656 | tf_op jit(solution)/shard_map/ppermute | solution.py:64
  43.7 11.6 %collective-permute-start.6 = (bf16[512,384]{1,0:T(8,128)(2,1)}, bf16[512,384]{1,0:T(8,128)(2,1)}, u32[]{:S(2)}, u32[]{:S(2)}) collective-permute-start(bf16[512,384]{1,0:T(8,128)(2,1)} %collective-permute-done.4.refs_4_), channel_id=1, source_target_pairs={{0,56},{4,60},{8,0},{12,4},{16,8},{20,12},{24,16},{28,20},{32,24},... | collective-permute-start | bytes 1179656 | tf_op jit(solution)/shard_map/ppermute | solution.py:64
  55.4 10.7 %collective-permute-start.12 = (bf16[512,384]{1,0:T(8,128)(2,1)}, bf16[512,384]{1,0:T(8,128)(2,1)S(1)}, u32[]{:S(2)}, u32[]{:S(2)}) collective-permute-start(bf16[512,384]{1,0:T(8,128)(2,1)} %collective-permute-done.5.refs_6_), channel_id=1, source_target_pairs={{0,8},{4,12},{8,16},{12,20},{16,24},{20,28},{24,32},{28,36},{32,40... | collective-permute-start | bytes 1179656 | tf_op jit(solution)/shard_map/ppermute | solution.py:64
  55.4 13.0 %collective-permute-start.14 = (bf16[512,384]{1,0:T(8,128)(2,1)}, bf16[512,384]{1,0:T(8,128)(2,1)S(1)}, u32[]{:S(2)}, u32[]{:S(2)}) collective-permute-start(bf16[512,384]{1,0:T(8,128)(2,1)} %collective-permute-done.6.refs_8_), channel_id=1, source_target_pairs={{0,56},{4,60},{8,0},{12,4},{16,8},{20,12},{24,16},{28,20},{32,24},... | collective-permute-start | bytes 1179656 | tf_op jit(solution)/shard_map/ppermute | solution.py:64
  58.1 10.4 %collective-permute-start.7 = (bf16[512,384]{1,0:T(8,128)(2,1)S(1)}, bf16[512,384]{1,0:T(8,128)(2,1)S(1)}, u32[]{:S(2)}, u32[]{:S(2)}) collective-permute-start(bf16[512,384]{1,0:T(8,128)(2,1)S(1)} %pad_maximum_fusion.1.refs_0_), channel_id=1, source_target_pairs={{0,4},{4,0},{8,12},{12,8},{16,20},{20,16},{24,28},{28,24},{32,36},... | collective-permute-start | bytes 1179656 | tf_op jit(solution)/shard_map/ppermute | solution.py:64
  60.1 8.8 %collective-permute-start.8 = (bf16[512,384]{1,0:T(8,128)(2,1)}, bf16[512,384]{1,0:T(8,128)(2,1)S(1)}, u32[]{:S(2)}, u32[]{:S(2)}) collective-permute-start(bf16[512,384]{1,0:T(8,128)(2,1)} %collective-permute-done.3.refs_2_), channel_id=1, source_target_pairs={{0,4},{4,0},{8,12},{12,8},{16,20},{20,16},{24,28},{28,24},{32,36},... | collective-permute-start | bytes 1179656 | tf_op jit(solution)/shard_map/ppermute | solution.py:64
  60.1 9.4 %collective-permute-start.9 = (bf16[512,384]{1,0:T(8,128)(2,1)}, bf16[512,384]{1,0:T(8,128)(2,1)S(1)}, u32[]{:S(2)}, u32[]{:S(2)}) collective-permute-start(bf16[512,384]{1,0:T(8,128)(2,1)} %collective-permute-done.4.refs_4_), channel_id=1, source_target_pairs={{0,4},{4,0},{8,12},{12,8},{16,20},{20,16},{24,28},{28,24},{32,36},... | collective-permute-start | bytes 1179656 | tf_op jit(solution)/shard_map/ppermute | solution.py:64
  66.1 3.9 %collective-permute-start.10 = (bf16[512,384]{1,0:T(8,128)(2,1)}, bf16[512,384]{1,0:T(8,128)(2,1)S(1)}, u32[]{:S(2)}, u32[]{:S(2)}) collective-permute-start(bf16[512,384]{1,0:T(8,128)(2,1)} %collective-permute-done.5.refs_6_), channel_id=1, source_target_pairs={{0,4},{4,0},{8,12},{12,8},{16,20},{20,16},{24,28},{28,24},{32,36},... | collective-permute-start | bytes 1179656 | tf_op jit(solution)/shard_map/ppermute | solution.py:64
  68.4 9.1 %collective-permute-start.11 = (bf16[512,384]{1,0:T(8,128)(2,1)}, bf16[512,384]{1,0:T(8,128)(2,1)S(1)}, u32[]{:S(2)}, u32[]{:S(2)}) collective-permute-start(bf16[512,384]{1,0:T(8,128)(2,1)} %collective-permute-done.6.refs_8_), channel_id=1, source_target_pairs={{0,4},{4,0},{8,12},{12,8},{16,20},{20,16},{24,28},{28,24},{32,36},... | collective-permute-start | bytes 1179656 | tf_op jit(solution)/shard_map/ppermute | solution.py:64
  68.5 7.4 %collective-permute-start.16 = (bf16[256,384]{1,0:T(8,128)(2,1)S(1)}, bf16[256,384]{1,0:T(8,128)(2,1)S(1)}, u32[]{:S(2)}, u32[]{:S(2)}) collective-permute-start(bf16[256,384]{1,0:T(8,128)(2,1)S(1)} %slice.18), channel_id=1, source_target_pairs={{0,8},{4,12},{8,16},{12,20},{16,24},{20,28},{24,32},{28,36},{32,40... | collective-permute-start | bytes 589832 | tf_op jit(solution)/shard_map/ppermute | solution.py:64
  68.8 8.6 %collective-permute-start.13 = (bf16[512,384]{1,0:T(8,128)(2,1)S(1)}, bf16[512,384]{1,0:T(8,128)(2,1)S(1)}, u32[]{:S(2)}, u32[]{:S(2)}) collective-permute-start(bf16[512,384]{1,0:T(8,128)(2,1)S(1)} %collective-permute-done.12.refs_10_), channel_id=1, source_target_pairs={{0,4},{4,0},{8,12},{12,8},{16,20},{20,16},{24,28},{28,24},{32,36},... | collective-permute-start | bytes 1179656 | tf_op jit(solution)/shard_map/ppermute | solution.py:64
  69.4 8.1 %collective-permute-start.15 = (bf16[512,384]{1,0:T(8,128)(2,1)S(1)}, bf16[512,384]{1,0:T(8,128)(2,1)S(1)}, u32[]{:S(2)}, u32[]{:S(2)}) collective-permute-start(bf16[512,384]{1,0:T(8,128)(2,1)S(1)} %collective-permute-done.14.refs_12_), channel_id=1, source_target_pairs={{0,4},{4,0},{8,12},{12,8},{16,20},{20,16},{24,28},{28,24},{32,36},... | collective-permute-start | bytes 1179656 | tf_op jit(solution)/shard_map/ppermute | solution.py:64
  69.9 7.4 %collective-permute-start.18 = (bf16[256,384]{1,0:T(8,128)(2,1)S(1)}, bf16[256,384]{1,0:T(8,128)(2,1)S(1)}, u32[]{:S(2)}, u32[]{:S(2)}) collective-permute-start(bf16[256,384]{1,0:T(8,128)(2,1)S(1)} %slice.19), channel_id=1, source_target_pairs={{0,56},{4,60},{8,0},{12,4},{16,8},{20,12},{24,16},{28,20},{32,24},... | collective-permute-start | bytes 589832 | tf_op jit(solution)/shard_map/ppermute | solution.py:64
  76.0 2.4 %collective-permute-start.17 = (bf16[256,384]{1,0:T(8,128)(2,1)S(1)}, bf16[256,384]{1,0:T(8,128)(2,1)S(1)}, u32[]{:S(2)}, u32[]{:S(2)}) collective-permute-start(bf16[256,384]{1,0:T(8,128)(2,1)S(1)} %collective-permute-done.16.refs_14_), channel_id=1, source_target_pairs={{0,4},{4,0},{8,12},{12,8},{16,20},{20,16},{24,28},{28,24},{32,36},... | collective-permute-start | bytes 589832 | tf_op jit(solution)/shard_map/ppermute | solution.py:64
  77.3 1.4 collective-permute-start.19
  85.6 37.3 %copy-start.4 = (bf16[1024,384]{1,0:T(8,128)(2,1)S(1)}, bf16[1024,384]{1,0:T(8,128)(2,1)}, u32[]{:S(2)}) copy-start(bf16[1024,384]{1,0:T(8,128)(2,1)} %copy-done.3) | copy-start | bytes 2359300
  129.8 1.7 copy-start.2
  131.4 43.6 %all-to-all-start.4 = ((bf16[8,512,384]{2,1,0:T(8,128)(2,1)}), bf16[8,512,384]{2,1,0:T(8,128)(2,1)}, u32[]{:S(2)}, u32[]{:S(2)}) async-start(bf16[8,512,384]{2,1,0:T(8,128)(2,1)} %bitcast.35), calls=%async_computation.4 | async-start | bytes 6291456 | tf_op jit(solution)/shard_map/all_to_all | solution.py:602
  140.4 2.3 %copy-start.9 = (bf16[1152,384]{0,1:T(8,128)(2,1)S(1)}, bf16[1152,384]{0,1:T(8,128)(2,1)}, u32[]{:S(2)}) copy-start(bf16[1152,384]{0,1:T(8,128)(2,1)} %copy-done.8) | copy-start | bytes 2654212
  144.1 39.5 %collective-permute-start.29 = (bf16[1024,288]{0,1:T(8,128)(2,1)}, bf16[1024,288]{0,1:T(8,128)(2,1)}, u32[]{:S(2)}, u32[]{:S(2)}) collective-permute-start(bf16[1024,288]{0,1:T(8,128)(2,1)} %convolution_convert_fusion.1), channel_id=1, source_target_pairs={{0,3},{1,0},{2,1},{3,2},{4,7},{5,4},{6,5},{7,6},{8,11},{9,8},{10,9... | collective-permute-start | bytes 1769480 | tf_op jit(solution)/shard_map/ppermute | solution.py:513
  148.2 38.3 %collective-permute-start.28 = (bf16[1024,288]{0,1:T(8,128)(2,1)}, bf16[1024,288]{0,1:T(8,128)(2,1)}, u32[]{:S(2)}, u32[]{:S(2)}) collective-permute-start(bf16[1024,288]{0,1:T(8,128)(2,1)} %convolution_convert_fusion.2), channel_id=1, source_target_pairs={{0,2},{1,3},{2,0},{3,1},{4,6},{5,7},{6,4},{7,5},{8,10},{9,11},{10,... | collective-permute-start | bytes 1769480 | tf_op jit(solution)/shard_map/ppermute | solution.py:513
  150.0 39.2 %collective-permute-start.27 = (bf16[1024,288]{0,1:T(8,128)(2,1)}, bf16[1024,288]{0,1:T(8,128)(2,1)}, u32[]{:S(2)}, u32[]{:S(2)}) collective-permute-start(bf16[1024,288]{0,1:T(8,128)(2,1)} %convolution_convert_fusion.3), channel_id=1, source_target_pairs={{0,1},{1,2},{2,3},{3,0},{4,5},{5,6},{6,7},{7,4},{8,9},{9,10},{10,1... | collective-permute-start | bytes 1769480 | tf_op jit(solution)/shard_map/ppermute | solution.py:513
  175.0 1.2 copy-start.1
  179.5 0.6 copy-start.6
  180.1 0.6 copy-start.7
  180.7 9.2 %collective-permute-start.26 = (bf16[128,384]{1,0:T(8,128)(2,1)}, bf16[128,384]{1,0:T(8,128)(2,1)}, u32[]{:S(2)}, u32[]{:S(2)}) collective-permute-start(bf16[128,384]{1,0:T(8,128)(2,1)} %get-tuple-element.62), channel_id=1, source_target_pairs={{0,56},{4,60},{8,0},{12,4},{16,8},{20,12},{24,16},{28,20},{32,24},... | collective-permute-start | bytes 294920 | tf_op jit(solution)/shard_map/ppermute | solution.py:64
  181.9 9.9 %collective-permute-start.25 = (bf16[128,384]{1,0:T(8,128)(2,1)}, bf16[128,384]{1,0:T(8,128)(2,1)}, u32[]{:S(2)}, u32[]{:S(2)}) collective-permute-start(bf16[128,384]{1,0:T(8,128)(2,1)} %get-tuple-element.61), channel_id=1, source_target_pairs={{0,48},{4,52},{8,56},{12,60},{16,0},{20,4},{24,8},{28,12},{32,16},... | collective-permute-start | bytes 294920 | tf_op jit(solution)/shard_map/ppermute | solution.py:64
  183.5 14.1 %collective-permute-start.24 = (bf16[128,384]{1,0:T(8,128)(2,1)}, bf16[128,384]{1,0:T(8,128)(2,1)}, u32[]{:S(2)}, u32[]{:S(2)}) collective-permute-start(bf16[128,384]{1,0:T(8,128)(2,1)} %copy-done.7), channel_id=1, source_target_pairs={{0,40},{4,44},{8,48},{12,52},{16,56},{20,60},{24,0},{28,4},{32,8},... | collective-permute-start | bytes 294920 | tf_op jit(solution)/shard_map/ppermute | solution.py:64
  186.5 11.4 %collective-permute-start.23 = (bf16[128,384]{1,0:T(8,128)(2,1)}, bf16[128,384]{1,0:T(8,128)(2,1)}, u32[]{:S(2)}, u32[]{:S(2)}) collective-permute-start(bf16[128,384]{1,0:T(8,128)(2,1)} %copy-done.6), channel_id=1, source_target_pairs={{0,32},{4,36},{8,40},{12,44},{16,48},{20,52},{24,56},{28,60},{32,0... | collective-permute-start | bytes 294920 | tf_op jit(solution)/shard_map/ppermute | solution.py:64
  189.2 14.3 %collective-permute-start.22 = (bf16[128,384]{1,0:T(8,128)(2,1)S(1)}, bf16[128,384]{1,0:T(8,128)(2,1)}, u32[]{:S(2)}, u32[]{:S(2)}) collective-permute-start(bf16[128,384]{1,0:T(8,128)(2,1)S(1)} %get-tuple-element.58), channel_id=1, source_target_pairs={{0,24},{4,28},{8,32},{12,36},{16,40},{20,44},{24,48},{28,52},{32,5... | collective-permute-start | bytes 294920 | tf_op jit(solution)/shard_map/ppermute | solution.py:64
  190.0 13.6 %collective-permute-start.21 = (bf16[128,384]{1,0:T(8,128)(2,1)S(1)}, bf16[128,384]{1,0:T(8,128)(2,1)}, u32[]{:S(2)}, u32[]{:S(2)}) collective-permute-start(bf16[128,384]{1,0:T(8,128)(2,1)S(1)} %get-tuple-element.57), channel_id=1, source_target_pairs={{0,16},{4,20},{8,24},{12,28},{16,32},{20,36},{24,40},{28,44},{32,4... | collective-permute-start | bytes 294920 | tf_op jit(solution)/shard_map/ppermute | solution.py:64
  191.8 15.4 %collective-permute-start.20 = (bf16[128,384]{1,0:T(8,128)(2,1)S(1)}, bf16[128,384]{1,0:T(8,128)(2,1)}, u32[]{:S(2)}, u32[]{:S(2)}) collective-permute-start(bf16[128,384]{1,0:T(8,128)(2,1)S(1)} %get-tuple-element.56), channel_id=1, source_target_pairs={{0,8},{4,12},{8,16},{12,20},{16,24},{20,28},{24,32},{28,36},{32,40... | collective-permute-start | bytes 294920 | tf_op jit(solution)/shard_map/ppermute | solution.py:64
  195.3 13.1 %copy-start.5 = (bf16[768,384]{1,0:T(8,128)(2,1)S(1)}, bf16[768,384]{1,0:T(8,128)(2,1)}, u32[]{:S(2)}) copy-start(bf16[768,384]{1,0:T(8,128)(2,1)} %pad_maximum_fusion.w_ref) | copy-start | bytes 1769476
where the time goes:
time: 224 us; the launch traced here: 222 us
  blocking collectives  58.8 us (26%)
  starting transfers between devices  51.8 us (23%)
  waiting for transfers between devices  49.4 us (22%)
  Pallas kernels  21.3 us (10%)
  local copies, waits for them, and re-layouts  20.8 us (9%)
  matrix products  11.5 us (5%)
  other arithmetic  7.16 us (3%)
    all_to_all x2, blocking collectives, body(): lax.all_to_all(stats, 'frames', split_axis=0, concat_axis=0, tiled=True)  36.9 us
    ppermute x27, starting transfers between devices, hop(): return lax.ppermute(value, 'frames', frames_perm(**shift))  33.9 us
    ppermute x27, waiting for transfers between devices, hop(): return lax.ppermute(value, 'frames', frames_perm(**shift))  23.6 us
    all_to_all x1, waiting for transfers between devices, body(): lax.all_to_all(partial.reshape(nx * nc, nz * cap * nq, 2 * cols), 'frames...  22.8 us
    all_to_all x1, blocking collectives, body(): lax.all_to_all(incoming, 'frames', 0, 0, axis_index_groups=flat, tiled=True)  11.4 us
    all_to_all x1, blocking collectives, body(): blocks = lax.all_to_all(blocks, 'mp', 0, 0, tiled=True)  10.5 us
    unnamed x41, local copies, waits for them, and re-layouts  9 us
    all_to_all x1, starting transfers between devices, body(): lax.all_to_all(passed, 'frames', 0, 0, axis_index_groups=line, tiled=True)  8.18 us
  transfers between devices with their start and end apart: 32, of which 11 were waited for; matrix products, arithmetic and copies ran while one was open for 12% of the time, Pallas kernels for 3%

commit v1 on v0

--- a/solution.py
+++ b/solution.py
@@ -242,17 +242,31 @@
         out_ref[...] = dot(pick_ref[to], rows, NN).astype(BF16)
 
 
-def project_kernel(x_ref, w_ref, out_ref, *, cols):
+def project_kernel(*refs, cols):
     lane = lax.broadcasted_iota(jnp.int32, (1, 256), 1)
-    grad = x_ref[:, 0:256] * (lane < cols).astype(BF16)
-    mixed = x_ref[:, 128:384] * (lane >= cols - 128).astype(BF16)
-    rows = x_ref.shape[0]
+    *parts, w_ref, out_ref = refs
+    total = parts[0][...].astype(F32)
+    for part_ref in parts[1:]:
+        total = total + part_ref[...].astype(F32)
+    total = total.astype(BF16)
+    grad = total[:, 0:256] * (lane < cols).astype(BF16)
+    mixed = total[:, 128:384] * (lane >= cols - 128).astype(BF16)
+    rows = total.shape[0]
     many = out_ref.shape[0]
     part = w_ref.shape[0] // many
     for to in range(many):
         at = pl.ds(to * part, part)
         out_ref[to, 0:rows, :] = dot(mixed, w_ref[at, 128:384], NT).astype(out_ref.dtype)
         out_ref[to, rows:2 * rows, :] = dot(grad, w_ref[at, 0:256], NT).astype(out_ref.dtype)
+
+
+def add_kernel(blocks_ref, att_ref, grad_ref):
+    rows = att_ref.shape[0]
+    for at, out_ref in ((0, att_ref), (rows, grad_ref)):
+        total = blocks_ref[0, at:at + rows, :].astype(F32)
+        for i in range(1, blocks_ref.shape[0]):
+            total = total + blocks_ref[i, at:at + rows, :].astype(F32)
+        out_ref[...] = total.astype(out_ref.dtype)
 
 
 def call(kernel, out_shape, ins, outs, scratch=(), mib=1):
@@ -628,20 +642,19 @@
     merged = call(merge_kernel, (mine_shape,) * nz, "svv", "v" * nz, mib=4)(
         lax.rem(lax.div(me, nc), nz).astype(jnp.int32).reshape(1), pick_sum, partial
     )
-    mine = merged[0].astype(F32)
-    for s in range(1, nz):
-        mine = mine + hop(merged[s], dz=s).astype(F32)
-    mine, frame_grad = lax.optimization_barrier((mine.astype(BF16), frame_grad))
+    parts = [merged[0]] + [hop(merged[s], dz=s) for s in range(1, nz)]
+    parts, frame_grad = lax.optimization_barrier((parts, frame_grad))
     blocks = call(
         functools.partial(project_kernel, cols=cols),
         jax.ShapeDtypeStruct((shards, 2 * quests * nq, part), BF16),
-        "vv",
+        "v" * (nz + 1),
         "v",
         mib=2,
-    )(mine, w_q_out)
+    )(*parts, w_q_out)
     blocks = lax.all_to_all(blocks, "mp", 0, 0, tiled=True)
-    both = jnp.sum(blocks.astype(F32), axis=0).astype(BF16).reshape(2, quests, nq, part)
-    return both[0], both[1], frame_grad
+    out = jax.ShapeDtypeStruct((quests * nq, part), BF16)
+    attended, query_grad = call(add_kernel, (out, out), "v", "vv")(blocks)
+    return attended.reshape(quests, nq, part), query_grad.reshape(quests, nq, part), frame_grad
 
 
 def solution(mesh):

time: 224 us -> 227 us (1.013)
  local copies, waits for them, and re-layouts: 20.8 us -> 26.5 us
  waiting for transfers between devices: 49.4 us -> 45.6 us
    unnamed x41 -> x65, local copies, waits for them, and re-layouts: 9 us -> 16.6 us
    ppermute x27, waiting for transfers between devices: 23.6 us -> 19.6 us  [hop(): return lax.ppermute(value, 'frames', frames_perm(**shift))]
  transfers between devices with their start and end apart: 32 -> 32, of which waited for: 11 -> 10; matrix products, arithmetic and copies ran while one was open for 12% -> 12% of each run, Pallas kernels for 3% -> 3%
where the time goes in v1:
time: 227 us; the launch traced here: 225 us
  blocking collectives  58.5 us (26%)
  starting transfers between devices  53.2 us (23%)
  waiting for transfers between devices  45.6 us (20%)
  local copies, waits for them, and re-layouts  26.5 us (12%)
  Pallas kernels  22.8 us (10%)
  matrix products  11.5 us (5%)
  other arithmetic  5.75 us (3%)
    all_to_all x2, blocking collectives, body(): lax.all_to_all(stats, 'frames', split_axis=0, concat_axis=0, tiled=True)  36.6 us
    ppermute x27, starting transfers between devices, hop(): return lax.ppermute(value, 'frames', frames_perm(**shift))  34.3 us
    all_to_all x1, waiting for transfers between devices, body(): lax.all_to_all(partial.reshape(nx * nc, nz * cap * nq, 2 * cols), 'frames...  22.8 us
    ppermute x27, waiting for transfers between devices, hop(): return lax.ppermute(value, 'frames', frames_perm(**shift))  19.6 us
    unnamed x65, local copies, waits for them, and re-layouts  16.6 us
    all_to_all x1, blocking collectives, body(): lax.all_to_all(incoming, 'frames', 0, 0, axis_index_groups=flat, tiled=True)  11.6 us
    all_to_all x1, blocking collectives, body(): blocks = lax.all_to_all(blocks, 'mp', 0, 0, tiled=True)  10.4 us
    all_to_all x1, starting transfers between devices, body(): lax.all_to_all(passed, 'frames', 0, 0, axis_index_groups=line, tiled=True)  8.18 us
  transfers between devices with their start and end apart: 32, of which 10 were waited for; matrix products, arithmetic and copies ran while one was open for 12% of the time, Pallas kernels for 3%

profile of v1, /device:TPU:1, one launch (start us, length us, event | category | flops | bytes accessed | tf_op | source)
XLA Modules:
  0.0 225.0 jit_solution(9793314529203644448)
XLA Ops:
  0.7 1.4 convolution_convert_fusion.4
  2.3 1.3 convolution_convert_fusion.5
  4.4 3.4 %collective-permute-start.2 = (bf16[128,384]{1,0:T(8,128)(2,1)S(1)}, bf16[128,384]{1,0:T(8,128)(2,1)S(1)}, u32[]{:S(2)}, u32[]{:S(2)}) collective-permute-start(bf16[128,384]{1,0:T(8,128)(2,1)S(1)} %pad_maximum_fusion.2), channel_id=1, source_target_pairs={{0,192},{4,196},{8,200},{12,204},{16,208},{20,212},{24,216},{28,22... | collective-permute-start | bytes 294920 | tf_op jit(solution)/shard_map/ppermute | solution.py:64
  10.1 0.7 copy.70
  10.8 8.2 %all-to-all-start = ((s32[8,1,16]{2,1,0:T(1,128)}), s32[8,1,16]{2,1,0:T(1,128)S(1)}, u32[]{:S(2)}, u32[]{:S(2)}) async-start(s32[8,1,16]{2,1,0:T(1,128)} %copy.70), calls=%async_computation | async-start | bytes 8192 | tf_op jit(solution)/shard_map/all_to_all | solution.py:570
  19.2 1.5 fusion.3.kv_ref
  21.3 1.1 pad_maximum_fusion.1.refs_0_
  22.4 3.1 %all-to-all-done = s32[8,1,16]{2,1,0:T(1,128)S(1)} async-done(((s32[8,1,16]{2,1,0:T(1,128)}), s32[8,1,16]{2,1,0:T(1,128)S(1)}, u32[]{:S(2)}, u32[]{:S(2)}) %all-to-all-start) | async-done | bytes 544 | tf_op jit(solution)/shard_map/all_to_all | solution.py:570
  25.8 2.4 %collective-permute-start.4 = (bf16[512,384]{1,0:T(8,128)(2,1)S(1)}, bf16[512,384]{1,0:T(8,128)(2,1)}, u32[]{:S(2)}, u32[]{:S(2)}) collective-permute-start(bf16[512,384]{1,0:T(8,128)(2,1)S(1)} %pad_maximum_fusion.1.refs_0_), channel_id=1, source_target_pairs={{0,56},{4,60},{8,0},{12,4},{16,8},{20,12},{24,16},{28,20},{32,24},... | collective-permute-start | bytes 1179656 | tf_op jit(solution)/shard_map/ppermute | solution.py:64
  28.2 0.7 copy.72
  28.9 0.8 copy.73
  29.7 11.6 %all_to_all.41 = s32[8,1,16]{2,1,0:T(1,128)} all-to-all(s32[8,1,16]{2,1,0:T(1,128)S(1)} %copy.74), channel_id=1, replica_groups={{0,4,64,68,128,132,192,196},{8,12,72,76,136,140,200,204},{16,20,80,84,1..., dimensions={0} | all-to-all | bytes 1024 | tf_op jit(solution)/shard_map/all_to_all | solution.py:573
  41.3 0.7 copy.75
  42.0 0.7 copy.76
  42.8 0.9 reshape.222.codes_ref
  43.8 2.7 %collective-permute-start.6 = (bf16[512,384]{1,0:T(8,128)(2,1)}, bf16[512,384]{1,0:T(8,128)(2,1)}, u32[]{:S(2)}, u32[]{:S(2)}) collective-permute-start(bf16[512,384]{1,0:T(8,128)(2,1)} %collective-permute-done.4.refs_4_), channel_id=1, source_target_pairs={{0,56},{4,60},{8,0},{12,4},{16,8},{20,12},{24,16},{28,20},{32,24},... | collective-permute-start | bytes 1179656 | tf_op jit(solution)/shard_map/ppermute | solution.py:64
  47.1 0.8 select_n.91
  47.9 0.8 copy.77
  48.7 3.6 %shard_map.103 = (s32[64]{0:T(128)S(1)}, s32[2]{0:T(128)S(1)}, s32[256]{0:T(256)S(1)}) custom-call(s32[128]{0:T(128)S(1)} %reshape.222.codes_ref, s32[1]{0:T(128)} %bitcast.13.me_ref), custom_call_target="tpu_custom_call" | custom-call | tf_op jit(solution)/shard_map/pallas_call | solution.py:579
  52.3 3.1 %collective-permute-done.5.refs_6_ = bf16[512,384]{1,0:T(8,128)(2,1)} collective-permute-done((bf16[512,384]{1,0:T(8,128)(2,1)}, bf16[512,384]{1,0:T(8,128)(2,1)}, u32[]{:S(2)}, u32[]{:S(2)}) %collective-permute-start.5) | collective-permute-done | bytes 393248 | tf_op jit(solution)/shard_map/ppermute | solution.py:64
  55.6 2.7 %collective-permute-start.14 = (bf16[512,384]{1,0:T(8,128)(2,1)}, bf16[512,384]{1,0:T(8,128)(2,1)S(1)}, u32[]{:S(2)}, u32[]{:S(2)}) collective-permute-start(bf16[512,384]{1,0:T(8,128)(2,1)} %collective-permute-done.6.refs_8_), channel_id=1, source_target_pairs={{0,56},{4,60},{8,0},{12,4},{16,8},{20,12},{24,16},{28,20},{32,24},... | collective-permute-start | bytes 1179656 | tf_op jit(solution)/shard_map/ppermute | solution.py:64
  58.2 2.0 collective-permute-start.7
  60.7 5.5 %collective-permute-done.12.refs_10_ = bf16[512,384]{1,0:T(8,128)(2,1)S(1)} collective-permute-done((bf16[512,384]{1,0:T(8,128)(2,1)}, bf16[512,384]{1,0:T(8,128)(2,1)S(1)}, u32[]{:S(2)}, u32[]{:S(2)}) %collective-permute-start.12) | collective-permute-done | bytes 393248 | tf_op jit(solution)/shard_map/ppermute | solution.py:64
  66.2 2.3 %collective-permute-start.10 = (bf16[512,384]{1,0:T(8,128)(2,1)}, bf16[512,384]{1,0:T(8,128)(2,1)S(1)}, u32[]{:S(2)}, u32[]{:S(2)}) collective-permute-start(bf16[512,384]{1,0:T(8,128)(2,1)} %collective-permute-done.5.refs_6_), channel_id=1, source_target_pairs={{0,4},{4,0},{8,12},{12,8},{16,20},{20,16},{24,28},{28,24},{32,36},... | collective-permute-start | bytes 1179656 | tf_op jit(solution)/shard_map/ppermute | solution.py:64
  70.1 2.4 %collective-permute-start.18 = (bf16[256,384]{1,0:T(8,128)(2,1)S(1)}, bf16[256,384]{1,0:T(8,128)(2,1)S(1)}, u32[]{:S(2)}, u32[]{:S(2)}) collective-permute-start(bf16[256,384]{1,0:T(8,128)(2,1)S(1)} %slice.9), channel_id=1, source_target_pairs={{0,56},{4,60},{8,0},{12,4},{16,8},{20,12},{24,16},{28,20},{32,24},... | collective-permute-start | bytes 589832 | tf_op jit(solution)/shard_map/ppermute | solution.py:64
  72.5 3.6 %collective-permute-done.16.refs_14_ = bf16[256,384]{1,0:T(8,128)(2,1)S(1)} collective-permute-done((bf16[256,384]{1,0:T(8,128)(2,1)S(1)}, bf16[256,384]{1,0:T(8,128)(2,1)S(1)}, u32[]{:S(2)}, u32[]{:S(2)}) %collective-permute-start.16) | collective-permute-done | bytes 196640 | tf_op jit(solution)/shard_map/ppermute | solution.py:64
  76.1 1.3 collective-permute-start.17
  77.6 0.9 collective-permute-done.17.refs_15_
  78.9 6.8 %shard_map.104 = (f32[64,8,128]{2,1,0:T(8,128)S(1)}, bf16[8192,384]{1,0:T(8,128)(2,1)S(1)}) custom-call(s32[64]{0:T(128)S(1)} %get-tuple-element.52.order_ref, s32[2]{0:T(128)S(1)} %get-tuple-element.53.size_ref, s32[256]{0:T(256)S(1)} %get-tuple-element.54.at_ref, bf16[1024,384]{1,0:T(8,128)(2,1)S(1)} %fusion.3.kv_ref, ...), custom_call_target="tpu_custom_call" | custom-call | tf_op jit(solution)/shard_map/pallas_call | solution.py:597
  85.8 18.8 %all_to_all.42.st_ref = f32[64,8,128]{2,1,0:T(8,128)S(1)} all-to-all(f32[64,8,128]{2,1,0:T(8,128)S(1)} %get-tuple-element.59), channel_id=1, replica_groups=mesh['frames'=64,'mp'=4] {'frames'}, dimensions={0} | all-to-all | bytes 524288 | tf_op jit(solution)/shard_map/all_to_all | solution.py:605
  104.9 17.8 %all_to_all.43.st_ref = f32[64,8,128]{2,1,0:T(8,128)S(1)} all-to-all(f32[64,8,128]{2,1,0:T(8,128)S(1)} %shard_map.105), channel_id=1, replica_groups=mesh['frames'=64,'mp'=4] {'frames'}, dimensions={0} | all-to-all | bytes 524288 | tf_op jit(solution)/shard_map/all_to_all | solution.py:607
  122.7 6.9 %shard_map.106 = (bf16[4096,384]{1,0:T(8,128)(2,1)S(1)}, bf16[1024,384]{1,0:T(8,128)(2,1)S(1)}) custom-call(s32[64]{0:T(128)S(1)} %get-tuple-element.52.order_ref, s32[2]{0:T(128)S(1)} %get-tuple-element.53.size_ref, s32[256]{0:T(256)S(1)} %get-tuple-element.54.at_ref, bf16[1024,384]{1,0:T(8,128)(2,1)S(1)} %copy-done.4, ...), custom_call_target="tpu_custom_call" | custom-call | tf_op jit(solution)/shard_map/pallas_call | solution.py:608
  129.6 1.7 copy-done.2
  131.3 6.9 %all-to-all-start.4 = ((bf16[8,512,384]{2,1,0:T(8,128)(2,1)}), bf16[8,512,384]{2,1,0:T(8,128)(2,1)}, u32[]{:S(2)}, u32[]{:S(2)}) async-start(bf16[8,512,384]{2,1,0:T(8,128)(2,1)} %bitcast.35), calls=%async_computation.4 | async-start | bytes 6291456 | tf_op jit(solution)/shard_map/all_to_all | solution.py:616
  138.2 1.1 copy.78
  139.4 1.9 copy.79
  141.3 2.1 pad_maximum_fusion.refs_8_
  143.5 1.4 convolution_convert_fusion.1
  144.9 2.7 %collective-permute-start.29 = (bf16[1024,288]{0,1:T(8,128)(2,1)}, bf16[1024,288]{0,1:T(8,128)(2,1)}, u32[]{:S(2)}, u32[]{:S(2)}) collective-permute-start(bf16[1024,288]{0,1:T(8,128)(2,1)} %convolution_convert_fusion.1), channel_id=1, source_target_pairs={{0,3},{1,0},{2,1},{3,2},{4,7},{5,4},{6,5},{7,6},{8,11},{9,8},{10,9... | collective-permute-start | bytes 1769480 | tf_op jit(solution)/shard_map/ppermute | solution.py:527
  147.7 1.4 convolution_convert_fusion.2
  149.4 1.4 convolution_convert_fusion.3
  150.8 0.7 collective-permute-start.27
  151.7 1.4 and_convert_fusion.pick_ref
  153.1 22.8 %all-to-all-done.4 = bf16[8,512,384]{2,1,0:T(8,128)(2,1)} async-done(((bf16[8,512,384]{2,1,0:T(8,128)(2,1)}), bf16[8,512,384]{2,1,0:T(8,128)(2,1)}, u32[]{:S(2)}, u32[]{:S(2)}) %all-to-all-start.4) | async-done | bytes 3145760 | tf_op jit(solution)/shard_map/all_to_all | solution.py:616
  175.9 1.2 copy-done.1
  177.2 3.1 %shard_map.107 = (bf16[128,384]{1,0:T(8,128)(2,1)S(1)}, bf16[128,384]{1,0:T(8,128)(2,1)}, bf16[128,384]{1,0:T(8,128)(2,1)}, bf16[128,384]{1,0:T(8,128)(2,1)}, bf...) custom-call(s32[1]{0:T(128)} %bitcast.me_ref, ...), custom_call_target="tpu_custom_call" | custom-call | tf_op jit(solution)/shard_map/pallas_call | solution.py:642
  183.5 1.1 collective-permute-start.20
  184.7 2.2 collective-permute-start.22
  186.8 3.5 %collective-permute-start.23 = (bf16[128,384]{1,0:T(8,128)(2,1)}, bf16[128,384]{1,0:T(8,128)(2,1)S(1)}, u32[]{:S(2)}, u32[]{:S(2)}) collective-permute-start(bf16[128,384]{1,0:T(8,128)(2,1)} %copy-done.19), channel_id=1, source_target_pairs={{0,32},{4,36},{8,40},{12,44},{16,48},{20,52},{24,56},{28,60},{32,0... | collective-permute-start | bytes 294920 | tf_op jit(solution)/shard_map/ppermute | solution.py:64
  190.3 1.0 collective-permute-start.24
  191.4 2.0 collective-permute-start.25
  193.4 2.0 collective-permute-start.26
  195.4 3.0 %fusion.2 = bf16[1024,288]{0,1:T(8,128)(2,1)} fusion(bf16[1024,384]{1,0:T(8,128)(2,1)S(1)} %get-tuple-element.72, bf16[1024,288]{0,1:T(8,128)(2,1)} %collective-permute-done.29, bf16[1024,288]{0,1:T(8,128)(2,1)} %collective-permute-done.28, bf16[1024,288]{0,1:T(8,128)(2,1)} %collective-permute-done.27, bf16[1152,384]{0,1:T(8,128)(2,1)} %copy-done.20, ...), kind=kOutput, calls=%fused_computation.5 | convolution fusion | flops 228556800 | bytes 3440644 | tf_op jit(solution)/shard_map/dot_general | solution.py:630
  198.5 2.3 %copy.80 = bf16[1024,288]{1,0:T(8,128)(2,1)} copy(bf16[1024,288]{0,1:T(8,128)(2,1)} %fusion.2) | data formatting | bytes 1179648 | tf_op jit(solution)/shard_map/convert_element_type | solution.py:639
  202.0 4.7 %collective-permute-done.25.refs_6_ = bf16[128,384]{1,0:T(8,128)(2,1)} collective-permute-done((bf16[128,384]{1,0:T(8,128)(2,1)}, bf16[128,384]{1,0:T(8,128)(2,1)}, u32[]{:S(2)}, u32[]{:S(2)}) %collective-permute-start.25) | collective-permute-done | bytes 98336 | tf_op jit(solution)/shard_map/ppermute | solution.py:64
  206.7 0.9 collective-permute-done.26.refs_7_
  207.7 0.9 copy-done.7
  208.6 0.9 copy-done.9
  209.4 0.9 copy-done.11
  210.3 0.9 copy-done.13
  211.2 0.9 copy-done.15
  212.1 1.4 shard_map.108
  213.7 10.4 %all_to_all.44 = bf16[4,256,192]{1,2,0:T(8,128)(2,1)S(1)} all-to-all(bf16[4,256,192]{1,2,0:T(8,128)(2,1)S(1)} %copy.81), channel_id=1, replica_groups=mesh['frames'=64,'mp'=4] {'mp'}, dimensions={0} | all-to-all | bytes 786432 | tf_op jit(solution)/shard_map/all_to_all | solution.py:654
  224.3 0.7 shard_map.109
  (122 shorter events, 13.9 us)
Async XLA Ops:
  0.6 18.5 %copy-start = (bf16[16,64,1152]{2,1,0:T(8,128)(2,1)S(1)}, bf16[16,64,1152]{2,1,0:T(8,128)(2,1)}, u32[]{:S(2)}) copy-start(bf16[16,64,1152]{2,1,0:T(8,128)(2,1)} %param.8) | copy-start | bytes 7077892
  0.6 8.3 %copy-start.29 = (s32[4,16]{1,0:T(4,128)S(1)}, s32[4,16]{1,0:T(4,128)}, u32[]{:S(2)}) copy-start(s32[4,16]{1,0:T(4,128)} %param.9) | copy-start | bytes 772
  0.7 18.3 %copy-start.26 = (bf16[1152,192]{0,1:T(8,128)(2,1)S(1)}, bf16[1152,192]{0,1:T(8,128)(2,1)}, u32[]{:S(2)}) copy-start(bf16[1152,192]{0,1:T(8,128)(2,1)} %param.12) | copy-start | bytes 1327108
  2.1 16.9 %copy-start.27 = (bf16[1152,192]{0,1:T(8,128)(2,1)S(1)}, bf16[1152,192]{0,1:T(8,128)(2,1)}, u32[]{:S(2)}) copy-start(bf16[1152,192]{0,1:T(8,128)(2,1)} %param.13) | copy-start | bytes 1327108
  2.2 16.9 %copy-start.22 = (bf16[128,192]{1,0:T(8,128)(2,1)}, bf16[128,192]{1,0:T(8,128)(2,1)S(1)}, u32[]{:S(2)}) copy-start(bf16[128,192]{1,0:T(8,128)(2,1)S(1)} %copy.68) | copy-start | bytes 147460
  3.7 0.6 copy-start.24
  4.4 16.2 %collective-permute-start.2 = (bf16[128,384]{1,0:T(8,128)(2,1)S(1)}, bf16[128,384]{1,0:T(8,128)(2,1)S(1)}, u32[]{:S(2)}, u32[]{:S(2)}) collective-permute-start(bf16[128,384]{1,0:T(8,128)(2,1)S(1)} %pad_maximum_fusion.2), channel_id=1, source_target_pairs={{0,192},{4,196},{8,200},{12,204},{16,208},{20,212},{24,216},{28,22... | collective-permute-start | bytes 294920 | tf_op jit(solution)/shard_map/ppermute | solution.py:64
  7.8 12.8 %collective-permute-start.1 = (bf16[128,384]{1,0:T(8,128)(2,1)S(1)}, bf16[128,384]{1,0:T(8,128)(2,1)}, u32[]{:S(2)}, u32[]{:S(2)}) collective-permute-start(bf16[128,384]{1,0:T(8,128)(2,1)S(1)} %pad_maximum_fusion.2), channel_id=1, source_target_pairs={{0,128},{4,132},{8,136},{12,140},{16,144},{20,148},{24,152},{28,15... | collective-permute-start | bytes 294920 | tf_op jit(solution)/shard_map/ppermute | solution.py:64
  8.3 13.0 %collective-permute-start = (bf16[128,384]{1,0:T(8,128)(2,1)S(1)}, bf16[128,384]{1,0:T(8,128)(2,1)}, u32[]{:S(2)}, u32[]{:S(2)}) collective-permute-start(bf16[128,384]{1,0:T(8,128)(2,1)S(1)} %pad_maximum_fusion.2), channel_id=1, source_target_pairs={{0,64},{4,68},{8,72},{12,76},{16,80},{20,84},{24,88},{28,92},{32,9... | collective-permute-start | bytes 294920 | tf_op jit(solution)/shard_map/ppermute | solution.py:64
  9.4 0.6 copy-start.30
  10.8 14.7 %all-to-all-start = ((s32[8,1,16]{2,1,0:T(1,128)}), s32[8,1,16]{2,1,0:T(1,128)S(1)}, u32[]{:S(2)}, u32[]{:S(2)}) async-start(s32[8,1,16]{2,1,0:T(1,128)} %copy.70), calls=%async_computation | async-start | bytes 8192 | tf_op jit(solution)/shard_map/all_to_all | solution.py:570
  19.1 1.5 copy-start.20
  19.1 2.2 copy-start.23
  19.1 2.2 copy-start.25
  20.6 65.1 %copy-start.3 = (bf16[1024,384]{1,0:T(8,128)(2,1)}, bf16[1024,384]{1,0:T(8,128)(2,1)S(1)}, u32[]{:S(2)}) copy-start(bf16[1024,384]{1,0:T(8,128)(2,1)S(1)} %fusion.3.kv_ref) | copy-start | bytes 2359300
  20.6 0.7 copy-start.28
  25.5 18.1 %collective-permute-start.3 = (bf16[512,384]{1,0:T(8,128)(2,1)S(1)}, bf16[512,384]{1,0:T(8,128)(2,1)}, u32[]{:S(2)}, u32[]{:S(2)}) collective-permute-start(bf16[512,384]{1,0:T(8,128)(2,1)S(1)} %pad_maximum_fusion.1.refs_0_), channel_id=1, source_target_pairs={{0,8},{4,12},{8,16},{12,20},{16,24},{20,28},{24,32},{28,36},{32,40... | collective-permute-start | bytes 1179656 | tf_op jit(solution)/shard_map/ppermute | solution.py:64
  25.8 17.9 %collective-permute-start.4 = (bf16[512,384]{1,0:T(8,128)(2,1)S(1)}, bf16[512,384]{1,0:T(8,128)(2,1)}, u32[]{:S(2)}, u32[]{:S(2)}) collective-permute-start(bf16[512,384]{1,0:T(8,128)(2,1)S(1)} %pad_maximum_fusion.1.refs_0_), channel_id=1, source_target_pairs={{0,56},{4,60},{8,0},{12,4},{16,8},{20,12},{24,16},{28,20},{32,24},... | collective-permute-start | bytes 1179656 | tf_op jit(solution)/shard_map/ppermute | solution.py:64
  43.7 11.7 %collective-permute-start.5 = (bf16[512,384]{1,0:T(8,128)(2,1)}, bf16[512,384]{1,0:T(8,128)(2,1)}, u32[]{:S(2)}, u32[]{:S(2)}) collective-permute-start(bf16[512,384]{1,0:T(8,128)(2,1)} %collective-permute-done.3.refs_2_), channel_id=1, source_target_pairs={{0,8},{4,12},{8,16},{12,20},{16,24},{20,28},{24,32},{28,36},{32,40... | collective-permute-start | bytes 1179656 | tf_op jit(solution)/shard_map/ppermute | solution.py:64
  43.8 11.6 %collective-permute-start.6 = (bf16[512,384]{1,0:T(8,128)(2,1)}, bf16[512,384]{1,0:T(8,128)(2,1)}, u32[]{:S(2)}, u32[]{:S(2)}) collective-permute-start(bf16[512,384]{1,0:T(8,128)(2,1)} %collective-permute-done.4.refs_4_), channel_id=1, source_target_pairs={{0,56},{4,60},{8,0},{12,4},{16,8},{20,12},{24,16},{28,20},{32,24},... | collective-permute-start | bytes 1179656 | tf_op jit(solution)/shard_map/ppermute | solution.py:64
  55.5 10.7 %collective-permute-start.12 = (bf16[512,384]{1,0:T(8,128)(2,1)}, bf16[512,384]{1,0:T(8,128)(2,1)S(1)}, u32[]{:S(2)}, u32[]{:S(2)}) collective-permute-start(bf16[512,384]{1,0:T(8,128)(2,1)} %collective-permute-done.5.refs_6_), channel_id=1, source_target_pairs={{0,8},{4,12},{8,16},{12,20},{16,24},{20,28},{24,32},{28,36},{32,40... | collective-permute-start | bytes 1179656 | tf_op jit(solution)/shard_map/ppermute | solution.py:64
  55.6 13.0 %collective-permute-start.14 = (bf16[512,384]{1,0:T(8,128)(2,1)}, bf16[512,384]{1,0:T(8,128)(2,1)S(1)}, u32[]{:S(2)}, u32[]{:S(2)}) collective-permute-start(bf16[512,384]{1,0:T(8,128)(2,1)} %collective-permute-done.6.refs_8_), channel_id=1, source_target_pairs={{0,56},{4,60},{8,0},{12,4},{16,8},{20,12},{24,16},{28,20},{32,24},... | collective-permute-start | bytes 1179656 | tf_op jit(solution)/shard_map/ppermute | solution.py:64
  58.2 10.4 %collective-permute-start.7 = (bf16[512,384]{1,0:T(8,128)(2,1)S(1)}, bf16[512,384]{1,0:T(8,128)(2,1)S(1)}, u32[]{:S(2)}, u32[]{:S(2)}) collective-permute-start(bf16[512,384]{1,0:T(8,128)(2,1)S(1)} %pad_maximum_fusion.1.refs_0_), channel_id=1, source_target_pairs={{0,4},{4,0},{8,12},{12,8},{16,20},{20,16},{24,28},{28,24},{32,36},... | collective-permute-start | bytes 1179656 | tf_op jit(solution)/shard_map/ppermute | solution.py:64
  60.2 8.8 %collective-permute-start.8 = (bf16[512,384]{1,0:T(8,128)(2,1)}, bf16[512,384]{1,0:T(8,128)(2,1)S(1)}, u32[]{:S(2)}, u32[]{:S(2)}) collective-permute-start(bf16[512,384]{1,0:T(8,128)(2,1)} %collective-permute-done.3.refs_2_), channel_id=1, source_target_pairs={{0,4},{4,0},{8,12},{12,8},{16,20},{20,16},{24,28},{28,24},{32,36},... | collective-permute-start | bytes 1179656 | tf_op jit(solution)/shard_map/ppermute | solution.py:64
  60.2 9.4 %collective-permute-start.9 = (bf16[512,384]{1,0:T(8,128)(2,1)}, bf16[512,384]{1,0:T(8,128)(2,1)S(1)}, u32[]{:S(2)}, u32[]{:S(2)}) collective-permute-start(bf16[512,384]{1,0:T(8,128)(2,1)} %collective-permute-done.4.refs_4_), channel_id=1, source_target_pairs={{0,4},{4,0},{8,12},{12,8},{16,20},{20,16},{24,28},{28,24},{32,36},... | collective-permute-start | bytes 1179656 | tf_op jit(solution)/shard_map/ppermute | solution.py:64
  66.2 3.9 %collective-permute-start.10 = (bf16[512,384]{1,0:T(8,128)(2,1)}, bf16[512,384]{1,0:T(8,128)(2,1)S(1)}, u32[]{:S(2)}, u32[]{:S(2)}) collective-permute-start(bf16[512,384]{1,0:T(8,128)(2,1)} %collective-permute-done.5.refs_6_), channel_id=1, source_target_pairs={{0,4},{4,0},{8,12},{12,8},{16,20},{20,16},{24,28},{28,24},{32,36},... | collective-permute-start | bytes 1179656 | tf_op jit(solution)/shard_map/ppermute | solution.py:64
  68.5 9.1 %collective-permute-start.11 = (bf16[512,384]{1,0:T(8,128)(2,1)}, bf16[512,384]{1,0:T(8,128)(2,1)S(1)}, u32[]{:S(2)}, u32[]{:S(2)}) collective-permute-start(bf16[512,384]{1,0:T(8,128)(2,1)} %collective-permute-done.6.refs_8_), channel_id=1, source_target_pairs={{0,4},{4,0},{8,12},{12,8},{16,20},{20,16},{24,28},{28,24},{32,36},... | collective-permute-start | bytes 1179656 | tf_op jit(solution)/shard_map/ppermute | solution.py:64
  68.7 7.4 %collective-permute-start.16 = (bf16[256,384]{1,0:T(8,128)(2,1)S(1)}, bf16[256,384]{1,0:T(8,128)(2,1)S(1)}, u32[]{:S(2)}, u32[]{:S(2)}) collective-permute-start(bf16[256,384]{1,0:T(8,128)(2,1)S(1)} %slice.8), channel_id=1, source_target_pairs={{0,8},{4,12},{8,16},{12,20},{16,24},{20,28},{24,32},{28,36},{32,40... | collective-permute-start | bytes 589832 | tf_op jit(solution)/shard_map/ppermute | solution.py:64
  69.0 8.6 %collective-permute-start.13 = (bf16[512,384]{1,0:T(8,128)(2,1)S(1)}, bf16[512,384]{1,0:T(8,128)(2,1)S(1)}, u32[]{:S(2)}, u32[]{:S(2)}) collective-permute-start(bf16[512,384]{1,0:T(8,128)(2,1)S(1)} %collective-permute-done.12.refs_10_), channel_id=1, source_target_pairs={{0,4},{4,0},{8,12},{12,8},{16,20},{20,16},{24,28},{28,24},{32,36},... | collective-permute-start | bytes 1179656 | tf_op jit(solution)/shard_map/ppermute | solution.py:64
  69.5 8.1 %collective-permute-start.15 = (bf16[512,384]{1,0:T(8,128)(2,1)S(1)}, bf16[512,384]{1,0:T(8,128)(2,1)S(1)}, u32[]{:S(2)}, u32[]{:S(2)}) collective-permute-start(bf16[512,384]{1,0:T(8,128)(2,1)S(1)} %collective-permute-done.14.refs_12_), channel_id=1, source_target_pairs={{0,4},{4,0},{8,12},{12,8},{16,20},{20,16},{24,28},{28,24},{32,36},... | collective-permute-start | bytes 1179656 | tf_op jit(solution)/shard_map/ppermute | solution.py:64
  70.1 7.4 %collective-permute-start.18 = (bf16[256,384]{1,0:T(8,128)(2,1)S(1)}, bf16[256,384]{1,0:T(8,128)(2,1)S(1)}, u32[]{:S(2)}, u32[]{:S(2)}) collective-permute-start(bf16[256,384]{1,0:T(8,128)(2,1)S(1)} %slice.9), channel_id=1, source_target_pairs={{0,56},{4,60},{8,0},{12,4},{16,8},{20,12},{24,16},{28,20},{32,24},... | collective-permute-start | bytes 589832 | tf_op jit(solution)/shard_map/ppermute | solution.py:64
  76.1 2.4 %collective-permute-start.17 = (bf16[256,384]{1,0:T(8,128)(2,1)S(1)}, bf16[256,384]{1,0:T(8,128)(2,1)S(1)}, u32[]{:S(2)}, u32[]{:S(2)}) collective-permute-start(bf16[256,384]{1,0:T(8,128)(2,1)S(1)} %collective-permute-done.16.refs_14_), channel_id=1, source_target_pairs={{0,4},{4,0},{8,12},{12,8},{16,20},{20,16},{24,28},{28,24},{32,36},... | collective-permute-start | bytes 589832 | tf_op jit(solution)/shard_map/ppermute | solution.py:64
  77.5 1.4 collective-permute-start.19
  85.7 37.0 %copy-start.4 = (bf16[1024,384]{1,0:T(8,128)(2,1)S(1)}, bf16[1024,384]{1,0:T(8,128)(2,1)}, u32[]{:S(2)}) copy-start(bf16[1024,384]{1,0:T(8,128)(2,1)} %copy-done.3) | copy-start | bytes 2359300
  129.6 1.7 copy-start.2
  131.3 44.6 %all-to-all-start.4 = ((bf16[8,512,384]{2,1,0:T(8,128)(2,1)}), bf16[8,512,384]{2,1,0:T(8,128)(2,1)}, u32[]{:S(2)}, u32[]{:S(2)}) async-start(bf16[8,512,384]{2,1,0:T(8,128)(2,1)} %bitcast.35), calls=%async_computation.4 | async-start | bytes 6291456 | tf_op jit(solution)/shard_map/all_to_all | solution.py:616
  141.3 2.2 copy-start.21
  144.9 39.8 %collective-permute-start.29 = (bf16[1024,288]{0,1:T(8,128)(2,1)}, bf16[1024,288]{0,1:T(8,128)(2,1)}, u32[]{:S(2)}, u32[]{:S(2)}) collective-permute-start(bf16[1024,288]{0,1:T(8,128)(2,1)} %convolution_convert_fusion.1), channel_id=1, source_target_pairs={{0,3},{1,0},{2,1},{3,2},{4,7},{5,4},{6,5},{7,6},{8,11},{9,8},{10,9... | collective-permute-start | bytes 1769480 | tf_op jit(solution)/shard_map/ppermute | solution.py:527
  149.1 37.8 %collective-permute-start.28 = (bf16[1024,288]{0,1:T(8,128)(2,1)}, bf16[1024,288]{0,1:T(8,128)(2,1)}, u32[]{:S(2)}, u32[]{:S(2)}) collective-permute-start(bf16[1024,288]{0,1:T(8,128)(2,1)} %convolution_convert_fusion.2), channel_id=1, source_target_pairs={{0,2},{1,3},{2,0},{3,1},{4,6},{5,7},{6,4},{7,5},{8,10},{9,11},{10,... | collective-permute-start | bytes 1769480 | tf_op jit(solution)/shard_map/ppermute | solution.py:527
  150.8 39.5 %collective-permute-start.27 = (bf16[1024,288]{0,1:T(8,128)(2,1)}, bf16[1024,288]{0,1:T(8,128)(2,1)}, u32[]{:S(2)}, u32[]{:S(2)}) collective-permute-start(bf16[1024,288]{0,1:T(8,128)(2,1)} %convolution_convert_fusion.3), channel_id=1, source_target_pairs={{0,1},{1,2},{2,3},{3,0},{4,5},{5,6},{6,7},{7,4},{8,9},{9,10},{10,1... | collective-permute-start | bytes 1769480 | tf_op jit(solution)/shard_map/ppermute | solution.py:527
  175.9 1.2 copy-start.1
  180.3 0.6 copy-start.6
  180.9 0.6 copy-start.16
  181.6 0.7 copy-start.17
  182.2 0.6 copy-start.18
  182.8 0.6 copy-start.19
  183.5 7.9 %collective-permute-start.20 = (bf16[128,384]{1,0:T(8,128)(2,1)}, bf16[128,384]{1,0:T(8,128)(2,1)S(1)}, u32[]{:S(2)}, u32[]{:S(2)}) collective-permute-start(bf16[128,384]{1,0:T(8,128)(2,1)} %get-tuple-element.65), channel_id=1, source_target_pairs={{0,8},{4,12},{8,16},{12,20},{16,24},{20,28},{24,32},{28,36},{32,40... | collective-permute-start | bytes 294920 | tf_op jit(solution)/shard_map/ppermute | solution.py:64
  184.5 8.9 %collective-permute-start.21 = (bf16[128,384]{1,0:T(8,128)(2,1)}, bf16[128,384]{1,0:T(8,128)(2,1)S(1)}, u32[]{:S(2)}, u32[]{:S(2)}) collective-permute-start(bf16[128,384]{1,0:T(8,128)(2,1)} %get-tuple-element.66), channel_id=1, source_target_pairs={{0,16},{4,20},{8,24},{12,28},{16,32},{20,36},{24,40},{28,44},{32,4... | collective-permute-start | bytes 294920 | tf_op jit(solution)/shard_map/ppermute | solution.py:64
  184.7 16.1 %collective-permute-start.22 = (bf16[128,384]{1,0:T(8,128)(2,1)}, bf16[128,384]{1,0:T(8,128)(2,1)S(1)}, u32[]{:S(2)}, u32[]{:S(2)}) collective-permute-start(bf16[128,384]{1,0:T(8,128)(2,1)} %get-tuple-element.67), channel_id=1, source_target_pairs={{0,24},{4,28},{8,32},{12,36},{16,40},{20,44},{24,48},{28,52},{32,5... | collective-permute-start | bytes 294920 | tf_op jit(solution)/shard_map/ppermute | solution.py:64
  186.8 14.5 %collective-permute-start.23 = (bf16[128,384]{1,0:T(8,128)(2,1)}, bf16[128,384]{1,0:T(8,128)(2,1)S(1)}, u32[]{:S(2)}, u32[]{:S(2)}) collective-permute-start(bf16[128,384]{1,0:T(8,128)(2,1)} %copy-done.19), channel_id=1, source_target_pairs={{0,32},{4,36},{8,40},{12,44},{16,48},{20,52},{24,56},{28,60},{32,0... | collective-permute-start | bytes 294920 | tf_op jit(solution)/shard_map/ppermute | solution.py:64
  190.3 11.7 %collective-permute-start.24 = (bf16[128,384]{1,0:T(8,128)(2,1)}, bf16[128,384]{1,0:T(8,128)(2,1)}, u32[]{:S(2)}, u32[]{:S(2)}) collective-permute-start(bf16[128,384]{1,0:T(8,128)(2,1)} %copy-done.18), channel_id=1, source_target_pairs={{0,40},{4,44},{8,48},{12,52},{16,56},{20,60},{24,0},{28,4},{32,8},... | collective-permute-start | bytes 294920 | tf_op jit(solution)/shard_map/ppermute | solution.py:64
  191.4 7.1 %copy-start.8 = (bf16[128,384]{1,0:T(8,128)(2,1)}, bf16[128,384]{1,0:T(8,128)(2,1)S(1)}, u32[]{:S(2)}) copy-start(bf16[128,384]{1,0:T(8,128)(2,1)S(1)} %collective-permute-done.20.refs_1_) | copy-start | bytes 294916
  191.4 15.4 %collective-permute-start.25 = (bf16[128,384]{1,0:T(8,128)(2,1)}, bf16[128,384]{1,0:T(8,128)(2,1)}, u32[]{:S(2)}, u32[]{:S(2)}) collective-permute-start(bf16[128,384]{1,0:T(8,128)(2,1)} %copy-done.17), channel_id=1, source_target_pairs={{0,48},{4,52},{8,56},{12,60},{16,0},{20,4},{24,8},{28,12},{32,16},... | collective-permute-start | bytes 294920 | tf_op jit(solution)/shard_map/ppermute | solution.py:64
  193.4 5.1 %copy-start.10 = (bf16[128,384]{1,0:T(8,128)(2,1)}, bf16[128,384]{1,0:T(8,128)(2,1)S(1)}, u32[]{:S(2)}) copy-start(bf16[128,384]{1,0:T(8,128)(2,1)S(1)} %collective-permute-done.21.refs_2_) | copy-start | bytes 294916
  193.4 14.3 %collective-permute-start.26 = (bf16[128,384]{1,0:T(8,128)(2,1)}, bf16[128,384]{1,0:T(8,128)(2,1)}, u32[]{:S(2)}, u32[]{:S(2)}) collective-permute-start(bf16[128,384]{1,0:T(8,128)(2,1)} %copy-done.16), channel_id=1, source_target_pairs={{0,56},{4,60},{8,0},{12,4},{16,8},{20,12},{24,16},{28,20},{32,24},... | collective-permute-start | bytes 294920 | tf_op jit(solution)/shard_map/ppermute | solution.py:64
  198.5 9.2 %copy-start.5 = (bf16[768,384]{1,0:T(8,128)(2,1)S(1)}, bf16[768,384]{1,0:T(8,128)(2,1)}, u32[]{:S(2)}) copy-start(bf16[768,384]{1,0:T(8,128)(2,1)} %pad_maximum_fusion.refs_8_) | copy-start | bytes 1769476
  200.7 0.6 copy-start.12
  201.4 0.6 copy-start.14
  207.7 0.9 copy-start.7
  208.6 0.9 copy-start.9
  209.4 0.9 copy-start.11
  210.3 0.9 copy-start.13
  211.2 0.9 copy-start.15
